TPU v7x, 256 devices: a whole 4x4x8 slice. The times are simulated.
256 devices in a mesh: sect: 4 (over z_hi), ctx: 8 (over z_lo, y), tp: 8 (over x, core).
Axes of the slice: x: 4, y: 4, z: 8 (z_hi: 4, z_lo: 2; z = z_hi * 2 + z_lo), core: 2. Of those that a mesh axis runs over, the one named last changes fastest.
Arguments:
- patches: bfloat16 [4096, 1280], P(('sect', 'ctx')), may hold values from -6 to 6
- patch_gain: float32 [1280], replicated, may hold values from 0.25 to 1.75
- patch_shift: float32 [1280], replicated, may hold values from -3 to 3
- encoder_up: bfloat16 [1280, 5120], P(None, 'tp'), may hold values from -0.15625 to 0.15625
- encoder_down: bfloat16 [5120, 1280], P('tp'), may hold values from -0.078125 to 0.078125
- proj_weight: bfloat16 [1280, 8192], P(None, 'tp'), may hold values from -0.15625 to 0.15625
- hidden_text: bfloat16 [8192, 8192], P(('sect', 'ctx'), 'tp'), may hold values from -180 to 180
- slot_source: int32 [64], P(('sect', 'ctx')), may hold values from 0 to 4, as said below
- norm_gain: float32 [8192], P('tp'), may hold values from 0.25 to 1.75
- kv_weight: bfloat16 [2048, 8192], P(None, 'tp'), may hold values from -0.0625 to 0.0625
- queries: bfloat16 [8192, 4096], P(('sect', 'ctx'), 'tp'), may hold values from -40 to 40
Outputs:
- attended: bfloat16 [8192, 4096], P(('sect', 'ctx'), 'tp')
Inputs may be any that keep to these rules, and one draw needn't show every extreme that they name: `slot_source`: for each ctx index, the slots of the blocks with that index carry each value 0 to 3 exactly once, all other slots 4.
All inputs are finite; a program needn't handle non-finite values.
Results may differ from a plain program's by a relative error of at most 0.019.
Values may be sent and summed in bfloat16 or wider, within the bound.
No kernel may reach another device: no remote copies, remote signals or barrier semaphores. Data moves between devices by JAX's collectives and lax.ppermute only.
A program may use at most 128 MiB of HBM per device.

v0:
```python
from functools import partial
import math

import jax
import jax.numpy as jnp
from jax import lax
from jax.sharding import PartitionSpec as P

D = 8192
HEAD = 128
Q_HEADS = 32
KV_HEADS = 8
PATCHES = 128


def layer_norm(values, norm_scale, norm_shift):
    widened = values.astype(jnp.float32)
    center = jnp.mean(widened, axis=-1, keepdims=True)
    spread = jnp.mean(jnp.square(widened - center), axis=-1, keepdims=True)
    return ((widened - center) * lax.rsqrt(spread + 1e-06) * norm_scale + norm_shift).astype(
        jnp.bfloat16
    )


def rotate_keys(keys_in, positions):
    half_size = keys_in.shape[-2] // 2
    frequencies = jnp.exp(
        jnp.arange(half_size, dtype=jnp.float32) * (-2.0 * math.log(500000.0) / (2 * half_size))
    )
    angles = positions[None, :] * frequencies[:, None]
    cosine_table = jnp.cos(angles)
    sine_table = jnp.sin(angles)
    first_half = keys_in[..., :half_size, :]
    second_half = keys_in[..., half_size:, :]
    return jnp.concatenate(
        [
            first_half * cosine_table - second_half * sine_table,
            second_half * cosine_table + first_half * sine_table,
        ],
        axis=-2,
    )


def attend_update(state_now, queries_blk, query_pos, keys_blk, values_blk, key_pos):
    running_max, running_sum, accumulated = state_now
    scale_value = queries_blk.shape[-1] ** (-0.5)
    scores = (
        jnp.einsum("rkgd,kdn->kgrn", queries_blk, keys_blk, preferred_element_type=jnp.float32)
        * scale_value
    )
    allowed = query_pos[:, None] >= key_pos[None, :]
    scores = jnp.where(allowed, scores, -jnp.inf)
    new_max = jnp.maximum(running_max, jnp.max(scores, axis=-1))
    weights = jnp.exp(scores - new_max[..., None])
    running_sum = jnp.sum(weights, axis=-1)
    mixed_rows = jnp.einsum(
        "kgrn,kdn->kgrd",
        weights.astype(jnp.bfloat16),
        values_blk,
        preferred_element_type=jnp.float32,
    )
    accumulated = mixed_rows
    return (new_max, running_sum, accumulated)


def keep_state(state_now):
    return state_now


def fold_step(states, fragment, first_index, groups):
    key_tile, value_tile = fragment
    key_pos = jnp.arange(key_tile.shape[2], dtype=jnp.int32)
    updated = []
    for group_entry, state_now in zip(groups, states):
        group_queries, group_first = group_entry
        row_count = group_queries.shape[0]
        query_pos = group_first + jnp.arange(row_count, dtype=jnp.int32)
        runner = partial(
            attend_update,
            queries_blk=group_queries,
            query_pos=query_pos,
            keys_blk=key_tile,
            values_blk=value_tile,
            key_pos=key_pos,
        )
        updated.append(
            lax.cond(first_index <= group_first + row_count - 1, runner, keep_state, state_now)
        )
    return tuple(updated)


def initial_state(kv_count, group_size, row_count):
    return (
        jnp.full((kv_count, group_size, row_count), -1e30, jnp.float32),
        jnp.zeros((kv_count, group_size, row_count), jnp.float32),
        jnp.zeros((kv_count, group_size, row_count, HEAD), jnp.float32),
    )


def finish_state(state_now):
    final_max, final_sum, final_acc = state_now
    result = final_acc / final_sum[..., None]
    return jnp.transpose(result, (2, 0, 1, 3)).reshape(result.shape[2], -1).astype(jnp.bfloat16)


def body(
    patches,
    patch_gain,
    patch_shift,
    encoder_up,
    encoder_down,
    proj_weight,
    hidden_text,
    slot_source,
    norm_gain,
    kv_weight,
    queries,
):
    normed_patches = layer_norm(patches, patch_gain, patch_shift)
    enc_hidden = jax.nn.gelu(
        jnp.dot(normed_patches, encoder_up, preferred_element_type=jnp.float32), approximate=False
    ).astype(jnp.bfloat16)
    partial_out = jnp.dot(enc_hidden, encoder_down, preferred_element_type=jnp.float32)
    summed_out = lax.psum(partial_out, "tp")
    encoded = (patches.astype(jnp.float32) + summed_out).astype(jnp.bfloat16)
    image_emb = jnp.dot(encoded, proj_weight, preferred_element_type=jnp.float32).astype(
        jnp.bfloat16
    )
    slot_total = slot_source.shape[0]
    slots_start = hidden_text.reshape(slot_total, PATCHES, hidden_text.shape[1])
    current = slots_start
    fragment = lax.all_gather(image_emb, "sect", axis=0, tiled=True)
    first_source = jnp.int32(0) // PATCHES
    for offset in range(fragment.shape[0] // PATCHES):
        chosen = (slot_source == first_source + offset)[:, None, None]
        current = jnp.where(
            chosen, fragment[offset * PATCHES : (offset + 1) * PATCHES][None], current
        )
    merged = current.reshape(hidden_text.shape)
    widened = merged.astype(jnp.float32)
    square_sums = lax.psum(jnp.sum(jnp.square(widened), axis=1), "tp")
    inverse = lax.rsqrt(square_sums / D + 1e-05)
    normed_hidden = (widened * inverse[:, None] * norm_gain[None, :]).astype(jnp.bfloat16)
    head_rows = kv_weight.shape[0] // lax.axis_size("tp")
    projected = lax.psum_scatter(
        lax.dot_general(
            kv_weight, normed_hidden, (((1,), (1,)), ((), ())), preferred_element_type=jnp.float32
        ),
        "tp",
        scatter_dimension=0,
        tiled=True,
    )
    row_total = queries.shape[0]
    kv_count = head_rows // (2 * HEAD)
    projected = projected.reshape(kv_count, 2, HEAD, row_total)
    block_number = lax.axis_index(("sect", "ctx"))
    first_position = block_number * row_total
    positions = (first_position + jnp.arange(row_total, dtype=jnp.int32)).astype(jnp.float32)
    rotated = rotate_keys(projected[:, 0], positions).astype(jnp.bfloat16)
    value_rows = projected[:, 1].astype(jnp.bfloat16)
    group_size = Q_HEADS // KV_HEADS
    grouped_queries = queries.reshape(row_total, kv_count, group_size, HEAD)
    groups = ((grouped_queries, first_position),)
    initial = tuple(
        [initial_state(kv_count, group_size, group_entry[0].shape[0]) for group_entry in groups]
    )
    folder = partial(fold_step, groups=groups)
    finals = folder(
        initial,
        (
            lax.all_gather(rotated, ("sect", "ctx"), axis=2, tiled=True),
            lax.all_gather(value_rows, ("sect", "ctx"), axis=2, tiled=True),
        ),
        jnp.int32(0),
    )
    results = [finish_state(state_now) for state_now in finals]
    return results[0]


def solution(mesh):
    in_specs = (
        P(("sect", "ctx"), None),
        P(),
        P(),
        P(None, "tp"),
        P("tp", None),
        P(None, "tp"),
        P(("sect", "ctx"), "tp"),
        P(("sect", "ctx")),
        P("tp"),
        P(None, "tp"),
        P(("sect", "ctx"), "tp"),
    )
    out_specs = P(("sect", "ctx"), "tp")
    return jax.shard_map(body, mesh=mesh, in_specs=in_specs, out_specs=out_specs, check_vma=False)
```

profile of v0, /device:TPU:224, one launch (start us, length us, event | category | flops | bytes accessed | tf_op | source)
XLA Modules:
  0.0 380.6 jit_solution(16793101043001423742)
XLA Ops:
  6.5 1.2 convert_reduce_fusion
  7.8 1.2 fusion.24
  9.0 4.4 %fusion.55 = f32[128,1280]{1,0:T(8,128)} fusion(bf16[640,1280]{1,0:T(8,128)(2,1)} %param.17, bf16[1280,640]{1,0:T(8,128)(2,1)} %param.16, bf16[128,1280]{1,0:T(8,128)(2,1)} %param.13, f32[1280]{0:T(1024)} %param.15, f32[1280]{0:T(1024)} %param.14, f32[128]{0:T(128)S(1)} %add_rsqrt_fusion.1, f32[128]{0:T(128)S(1)} %broadcast_multiply_fusion), kind=kOutput, calls=%fused_computation.67 | convolution fusion | flops 425738240 | bytes 4271104 | tf_op jit(solution)/shard_map/dot_general | solution.py:123
  13.5 66.9 %all-reduce.2.cloned.1.call-done = f32[128,1280]{1,0:T(8,128)} async-done(((f32[128,1280]{1,0:T(8,128)}), f32[128,1280]{1,0:T(8,128)}) %all-reduce.2.cloned.1.call-update) | async-done | bytes 655376 | tf_op jit(solution)/shard_map/psum | solution.py:124
  80.4 2.3 convolution_convert_fusion
  83.0 32.8 %all-gather.5.cloned.1.call-done = bf16[512,1024]{1,0:T(8,128)(2,1)} async-done(((bf16[128,1024]{1,0:T(8,128)(2,1)}), bf16[512,1024]{1,0:T(8,128)(2,1)}) %all-gather.5.cloned.1.call-update) | async-done | bytes 1048592 | tf_op jit(solution)/shard_map/all_gather | solution.py:132
  115.8 1.3 fusion.127
  117.1 1.6 fusion.19
  118.6 14.5 %psum.15 = f32[256]{0:T(256)S(1)} all-reduce(f32[256]{0:T(256)S(1)} %get-tuple-element.38), channel_id=1, replica_groups=mesh['sect'=4,'ctx'=8,'tp'=8] {'tp'}, use_global_device_ids=true, to_apply=%region_4.5 | all-reduce | flops 256 | bytes 2048 | tf_op jit(solution)/shard_map/psum | solution.py:141
  133.2 5.1 %convolution_bitcast_fusion = f32[2048,256]{0,1:T(8,128)} fusion(bf16[2048,1024]{1,0:T(8,128)(2,1)} %param.22, bf16[256,1024]{1,0:T(8,128)(2,1)} %get-tuple-element.39, f32[1024]{0:T(1024)S(1)} %copy-done.6, f32[256]{0:T(256)S(1)} %add_rsqrt_fusion), kind=kOutput, calls=%fused_computation.19 | convolution fusion | flops 1074790400 | bytes 6820864 | tf_op jit(solution)/shard_map/dot_general | solution.py:146
  138.4 32.8 %reduce-scatter.2.cloned.1.call-done = f32[256,256]{0,1:T(8,128)} async-done(((f32[2048,256]{0,1:T(8,128)}), f32[256,256]{0,1:T(8,128)}) %reduce-scatter.2.cloned.1.call-update) | async-done | bytes 262160 | tf_op jit(solution)/shard_map/reduce_scatter | solution.py:145
  171.2 1.1 copy.20
  172.3 0.3 fusion.93
  172.6 0.6 pad_maximum_fusion
  173.2 0.2 all-gather.9.cloned.1.call-start
  173.5 0.6 slice.47
  174.1 72.5 %all-gather.7.cloned.1.call-done = bf16[1,128,8192]{2,1,0:T(8,128)(2,1)} async-done(((bf16[1,128,256]{2,1,0:T(8,128)(2,1)}), bf16[1,128,8192]{2,1,0:T(8,128)(2,1)}) %all-gather.7.cloned.1.call-update) | async-done | bytes 2097168 | tf_op jit(solution)/shard_map/all_gather | solution.py:171
  246.6 76.4 %all-gather.9.cloned.1.call-done = bf16[1,1,128,8192]{3,2,1,0:T(8,128)(2,1)} async-done(((bf16[1,1,128,256]{3,2,1,0:T(8,128)(2,1)}), bf16[1,1,128,8192]{3,2,1,0:T(8,128)(2,1)}) %all-gather.9.cloned.1.call-update) | async-done | bytes 2097168 | tf_op jit(solution)/shard_map/all_gather | solution.py:172
  323.0 49.8 %conditional.1 = (f32[1,4,256]{2,1,0:T(4,128)S(1)}, f32[1,4,256,128]{3,2,1,0:T(8,128)S(1)}) conditional(s32[]{:T(128)} %convert_element_type.65, () %tuple.13, (s32[]{:T(128)}, s32[256]{0:T(256)S(1)}, s32[8192]{0:T(1024)S(1)}, bf16[1,128,8192]{2,1,0:T(8,128)(2,1)}, bf16[256,512]{1,0:T(8,128)(2,1)S(1)}, ...), branch_computations={%region_6.7_spmd, %region_7.10_spmd} | conditional | flops 4389338112 | bytes 122481712 | solution.py:87
  323.0 3.7 broadcast_compare_fusion
  326.8 15.6 %fusion.2 = (f32[4,256]{1,0:T(4,128)S(1)}, f32[8192,256,4]{1,0,2:T(8,128)}) fusion(pred[256,8192]{0,1:T(8,128)(4,1)S(1)} %broadcast_compare_fusion, bf16[1,128,8192]{2,1,0:T(8,128)(2,1)} %get-tuple-element.35, bf16[256,512]{1,0:T(8,128)(2,1)S(1)} %get-tuple-element.31), kind=kOutput, calls=%fused_computation.4 | convolution fusion | flops 2172648448 | bytes 38014976 | tf_op jit(solution)/shard_map/cond/branch_1_fun/rkgd,kdn->kgrn/dot_general | solution.py:48
  342.4 15.8 %fusion.10 = f32[1,4,256,128]{3,2,1,0:T(8,128)S(1)} fusion(bf16[1,128,8192]{2,1,0:T(8,128)(2,1)} %get-tuple-element.25, f32[8192,256,4]{1,0,2:T(8,128)} %get-tuple-element.41, f32[4,256]{1,0:T(4,128)S(1)} %broadcast_maximum_fusion, pred[256,8192]{0,1:T(8,128)(4,1)} %copy-done.1), kind=kOutput, calls=%fused_computation.12 | convolution fusion | flops 2181038080 | bytes 38277120 | tf_op jit(solution)/shard_map/cond/branch_1_fun/kgrn,kdn->kgrd/dot_general | solution.py:56
  358.2 14.6 %fusion.1 = f32[4,256]{1,0:T(4,128)S(1)} fusion(f32[8192,256,4]{1,0,2:T(8,128)} %get-tuple-element.41, f32[4,256]{1,0:T(4,128)S(1)} %broadcast_maximum_fusion, pred[256,8192]{0,1:T(8,128)(4,1)} %copy-done.1), kind=kLoop, calls=%fused_computation.3 | loop fusion | flops 33553408 | bytes 35659776 | tf_op jit(solution)/shard_map/cond/branch_1_fun/reduce_sum | solution.py:55
  373.3 0.7 copy.33
  (38 shorter events, 0.9 us)
Async XLA Ops:
  6.5 73.9 %copy-start = (bf16[1280,1024]{1,0:T(8,128)(2,1)S(1)}, bf16[1280,1024]{1,0:T(8,128)(2,1)}, u32[]{:S(2)}) copy-start(bf16[1280,1024]{1,0:T(8,128)(2,1)} %param.18) | copy-start | bytes 7864324
  6.5 73.9 %all-reduce.2.cloned.1.call-start = ((), (), s32[]{:S(2)}) async-start(), calls=%async_computation.1 | async-start | bytes 1310720 | tf_op jit(solution)/shard_map/psum | solution.py:124
  9.0 71.4 %copy-start.2 = (bf16[128,1280]{1,0:T(8,128)(2,1)S(1)}, bf16[128,1280]{1,0:T(8,128)(2,1)}, u32[]{:S(2)}) copy-start(bf16[128,1280]{1,0:T(8,128)(2,1)} %param.13) | copy-start | bytes 983044
  13.5 69.3 %copy-start.4 = (s32[2]{0:T(128)S(1)}, s32[2]{0:T(128)}, u32[]{:S(2)}) copy-start(s32[2]{0:T(128)} %param.20) | copy-start | bytes 28
  13.5 103.6 %copy-start.3 = (bf16[256,1024]{1,0:T(8,128)(2,1)S(1)}, bf16[256,1024]{1,0:T(8,128)(2,1)}, u32[]{:S(2)}) copy-start(bf16[256,1024]{1,0:T(8,128)(2,1)} %param.19) | copy-start | bytes 1572868
  13.5 119.7 %copy-start.6 = (f32[1024]{0:T(1024)S(1)}, f32[1024]{0:T(1024)}, u32[]{:S(2)}) copy-start(f32[1024]{0:T(1024)} %param.21) | copy-start | bytes 12292
  13.5 102.3 %all-gather.5.cloned.1.call-start = ((), (), s32[]{:S(2)}) async-start(), calls=%async_computation.2 | async-start | bytes 1310720 | tf_op jit(solution)/shard_map/all_gather | solution.py:132
  82.7 88.4 %reduce-scatter.2.cloned.1.call-start = ((), (), s32[]{:S(2)}) async-start(), calls=%async_computation.3 | async-start | bytes 2359296 | tf_op jit(solution)/shard_map/reduce_scatter | solution.py:145
  133.2 189.9 %copy-start.5 = (bf16[256,512]{1,0:T(8,128)(2,1)S(1)}, bf16[256,512]{1,0:T(8,128)(2,1)}, u32[]{:S(2)}) copy-start(bf16[256,512]{1,0:T(8,128)(2,1)} %param.23) | copy-start | bytes 786436
  138.3 108.3 %all-gather.7.cloned.1.call-start = ((), (), s32[]{:S(2)}) async-start(), calls=%async_computation.4 | async-start | bytes 2162688 | tf_op jit(solution)/shard_map/all_gather | solution.py:171
  173.2 149.8 %all-gather.9.cloned.1.call-start = ((), (), s32[]{:S(2)}) async-start(), calls=%async_computation.5 | async-start | bytes 2162688 | tf_op jit(solution)/shard_map/all_gather | solution.py:172
  326.8 15.6 %copy-start.1 = (pred[256,8192]{0,1:T(8,128)(4,1)}, pred[256,8192]{0,1:T(8,128)(4,1)S(1)}, u32[]{:S(2)}) copy-start(pred[256,8192]{0,1:T(8,128)(4,1)S(1)} %broadcast_compare_fusion) | copy-start | bytes 6291460 | tf_op jit(solution)/shard_map/cond
Sparse Core Ops, SparseCore 0:
  13.6 66.7 all-reduce.1
  82.9 32.8 all-gather.4
  138.4 32.7 reduce-scatter.1
  173.5 73.0 all-gather.6
  248.9 74.0 all-gather.8
where the time goes:
time: 384 us; the launch traced here: 381 us
  waiting for transfers between devices  281 us (73%)
  matrix products  43.2 us (11%)
  other arithmetic  23.6 us (6%)
  blocking collectives  14.5 us (4%)
  between operations  13.3 us (3%)
  local copies, waits for them, and re-layouts  4.12 us (1%)
    all_gather x1, waiting for transfers between devices, body(): lax.all_gather(value_rows, ('sect', 'ctx'), axis=2, tiled=True)  76.4 us
    all_gather x1, waiting for transfers between devices, body(): lax.all_gather(rotated, ('sect', 'ctx'), axis=2, tiled=True)  72.5 us
    psum x1, waiting for transfers between devices, body(): summed_out = lax.psum(partial_out, 'tp')  66.9 us
    all_gather x1, waiting for transfers between devices, body(): fragment = lax.all_gather(image_emb, 'sect', axis=0, tiled=True)  32.8 us
    reduce_scatter x1, waiting for transfers between devices, body(): lax.psum_scatter(lax.dot_general(kv_weight, normed_hidden, (((1,), (1,)),...  32.8 us
    dot_general x1, matrix products, attend_update(): jnp.einsum('kgrn,kdn->kgrd', weights.astype(jnp.bfloat16), values_blk, pr...  15.8 us
    dot_general x1, matrix products, attend_update(): jnp.einsum('rkgd,kdn->kgrn', queries_blk, keys_blk, preferred_element_typ...  15.6 us
    reduce_sum x1, other arithmetic, attend_update(): running_sum = jnp.sum(weights, axis=-1)  14.6 us
  transfers between devices with their start and end apart: 5, of which 5 were waited for; matrix products, arithmetic and copies ran while one was open for 0% of the time, Pallas kernels for 0%

commit v1 on v0

v1 whole, which is shorter than its diff:
```python
import functools
import math

import jax
import jax.numpy as jnp
from jax import lax
from jax.experimental import pallas as pl
from jax.experimental.pallas import tpu as pltpu
from jax.sharding import Mesh
from jax.sharding import PartitionSpec as P

D = 8192
HEAD = 128
HALF = 64
GROUP = 4
TOK = 256
IMG = 128
ROWS = 272
TP = ("x", "core")
Z = ("zh", "zl")
BF16 = jnp.bfloat16
F32 = jnp.float32
NEG = -1e30
LOG2E = math.log2(math.e)
SCALE = HEAD ** (-0.5)


def shift(values, axis, step):
    count = lax.axis_size(axis)
    return lax.ppermute(values, axis, [(i, (i + step) % count) for i in range(count)])


def pick(values, index):
    return lax.dynamic_index_in_dim(values, index, 0, keepdims=False)


def tp_reduce_scatter(pieces):
    core, x_at = lax.axis_index("core"), lax.axis_index("x")
    pairs = jnp.swapaxes(pieces, 0, 1)
    got = shift(pick(pairs, 1 - core), "core", 1)
    summed = pick(pairs, core).astype(F32) + got.astype(F32)
    sent = summed.astype(BF16)
    total = pick(summed, x_at)
    for step in (2, 1, 3):
        total = total + shift(pick(sent, (x_at + step) % 4), "x", step).astype(F32)
    return total


def tp_all_gather(piece):
    core, x_at = lax.axis_index("core"), lax.axis_index("x")
    whole = jnp.zeros((4, *piece.shape), piece.dtype)
    whole = lax.dynamic_update_index_in_dim(whole, piece, x_at, 0)
    for step in (2, 1, 3):
        whole = lax.dynamic_update_index_in_dim(
            whole, shift(piece, "x", step), (x_at - step) % 4, 0
        )
    other = shift(whole, "core", 1)
    even = jnp.where(core == 0, whole, other)
    odd = jnp.where(core == 0, other, whole)
    return jnp.stack([even, odd], 1)


def layer_norm(values, norm_scale, norm_shift):
    widened = values.astype(F32)
    center = jnp.mean(widened, axis=-1, keepdims=True)
    spread = jnp.mean(jnp.square(widened - center), axis=-1, keepdims=True)
    return ((widened - center) * lax.rsqrt(spread + 1e-06) * norm_scale + norm_shift).astype(BF16)


def project(features, norm_gain, kv_weight):
    widened = features.astype(F32)
    squares = jnp.sum(jnp.square(widened), axis=1)
    gained = (widened * norm_gain[None, :]).astype(BF16)
    rows = lax.dot_general(
        kv_weight, gained, (((1,), (1,)), ((), ())), preferred_element_type=F32
    )
    return rows, squares


def attend_kernel(place, text_ref, image_ref, cos_ref, sin_ref, query_ref, out_ref, keys, values, scores, top):
    z_at, y_at = place[0], place[1]
    turn = pl.program_id(0)

    @pl.when(turn == 0)
    def merge():
        values[HEAD:, :] = jnp.ones((HEAD, 8 * TOK), BF16)
        for block in range(8):
            for slot in range(2):
                lanes = slice(slot * IMG, (slot + 1) * IMG)
                place_at = block * TOK + slot * IMG
                text = text_ref[block, :, lanes].astype(F32)
                source = text[TOK : TOK + 1, :]
                rows = text[:TOK, :]
                for r in range(4):
                    rows = jnp.where(
                        source == float(r), image_ref[2 * r + block % 2].astype(F32), rows
                    )
                cosine = cos_ref[:, place_at : place_at + IMG]
                sine = sin_ref[:, place_at : place_at + IMG]
                first, second = rows[:HALF], rows[HALF:HEAD]
                keys[:HALF, place_at : place_at + IMG] = (first * cosine - second * sine).astype(BF16)
                keys[HALF:, place_at : place_at + IMG] = (second * cosine + first * sine).astype(BF16)
                values[:HEAD, place_at : place_at + IMG] = rows[HEAD:].astype(BF16)

    block_at = lax.rem(y_at + 2 + turn, 4)
    queries = query_ref[...]
    full = z_at + jnp.where(y_at < block_at, 1, 0)
    count = z_at + jnp.where(y_at <= block_at, 1, 0)
    row_at = lax.broadcasted_iota(jnp.int32, (TOK, TOK), 0)
    lane_at = lax.broadcasted_iota(jnp.int32, (TOK, TOK), 1)
    allowed = row_at >= lane_at
    top[...] = jnp.full(top.shape, NEG, F32)

    def score(block, masked):
        at = pl.ds(pl.multiple_of(block * TOK, TOK), TOK)
        keys_now = keys[:, at]
        for h in range(GROUP):
            s = jnp.dot(
                queries[:, h * HEAD : (h + 1) * HEAD], keys_now, preferred_element_type=F32
            )
            if masked:
                s = jnp.where(allowed, s, -jnp.inf)
            scores[h, :, at] = s
            top[h] = jnp.maximum(top[h], jnp.maximum(s[:, :HEAD], s[:, HEAD:]))

    pl.loop(0, full)(lambda block: score(block, False))

    @pl.when(count > full)
    def diagonal():
        score(full, True)

    lane = lax.broadcasted_iota(jnp.int32, (TOK, HEAD), 1)
    stats = jnp.zeros((TOK, HEAD), F32)
    for h in range(GROUP):
        most = jnp.max(top[h], axis=1, keepdims=True)
        offset = most * (SCALE * LOG2E)

        def weigh(block, acc):
            at = pl.ds(pl.multiple_of(block * TOK, TOK), TOK)
            weights = jnp.exp2(scores[h, :, at] * (SCALE * LOG2E) - offset).astype(BF16)
            return acc + lax.dot_general(
                weights, values[:, at], (((1,), (1,)), ((), ())), preferred_element_type=F32
            )

        acc = lax.fori_loop(0, count, weigh, jnp.zeros((TOK, 2 * HEAD), F32))
        total = acc[:, HEAD : HEAD + 1]
        some = total > 0.0
        out_ref[0, :TOK, h * HEAD : (h + 1) * HEAD] = (
            acc[:, :HEAD] / jnp.where(some, total, 1.0)
        ).astype(BF16)
        level = jnp.where(some, offset + jnp.log2(jnp.where(some, total, 1.0)), NEG)
        for part in range(3):
            piece = level.astype(BF16).astype(F32)
            stats = jnp.where(lane == 3 * h + part, piece, stats)
            level = level - piece
    out_ref[0, TOK:, :TOK] = stats.T[: ROWS - TOK].astype(BF16)
    out_ref[0, TOK:, TOK:] = jnp.zeros((ROWS - TOK, 2 * HEAD), BF16)


def attend(place, text, images, cosine, sine, queries):
    def query_block(turn, place):
        return (lax.rem(place[1] + 2 + turn, 4), 0)

    whole = lambda rank: lambda turn, place: (0,) * rank
    return pl.pallas_call(
        attend_kernel,
        out_shape=jax.ShapeDtypeStruct((4, ROWS, GROUP * HEAD), BF16),
        grid_spec=pltpu.PrefetchScalarGridSpec(
            num_scalar_prefetch=1,
            grid=(4,),
            in_specs=[
                pl.BlockSpec(text.shape, whole(3)),
                pl.BlockSpec(images.shape, whole(3)),
                pl.BlockSpec(cosine.shape, whole(2)),
                pl.BlockSpec(sine.shape, whole(2)),
                pl.BlockSpec((TOK, GROUP * HEAD), query_block),
            ],
            out_specs=pl.BlockSpec((1, ROWS, GROUP * HEAD), lambda turn, place: (turn, 0, 0)),
            scratch_shapes=[
                pltpu.VMEM((HEAD, 8 * TOK), BF16),
                pltpu.VMEM((2 * HEAD, 8 * TOK), BF16),
                pltpu.VMEM((GROUP, TOK, 8 * TOK), F32),
                pltpu.VMEM((GROUP, TOK, HEAD), F32),
            ],
        ),
        compiler_params=pltpu.CompilerParams(vmem_limit_bytes=40 * 1024 * 1024),
        name="attend",
    )(place, text, images, cosine, sine, queries)


def combine_kernel(*refs):
    out_ref = refs[-1]
    levels = []
    for ref in refs[:-1]:
        rows = ref[TOK:, :TOK].astype(F32)
        levels.append(jnp.concatenate([rows, jnp.zeros((HEAD - rows.shape[0], TOK), F32)], 0).T)
    for h in range(GROUP):
        lanes = slice(h * HEAD, (h + 1) * HEAD)
        level = [
            l[:, 3 * h : 3 * h + 1] + l[:, 3 * h + 1 : 3 * h + 2] + l[:, 3 * h + 2 : 3 * h + 3]
            for l in levels
        ]
        most = functools.reduce(jnp.maximum, level)
        weights = [jnp.exp2(l - most) for l in level]
        total = sum(weights)
        mixed = sum(w * ref[:TOK, lanes].astype(F32) for w, ref in zip(weights, refs[:-1]))
        out_ref[:, lanes] = (mixed / total).astype(BF16)


def combine(parts):
    return pl.pallas_call(
        combine_kernel,
        out_shape=jax.ShapeDtypeStruct((TOK, GROUP * HEAD), BF16),
        name="combine",
    )(*parts)


def body(
    patches,
    patch_gain,
    patch_shift,
    encoder_up,
    encoder_down,
    proj_weight,
    hidden_text,
    slot_source,
    norm_gain,
    kv_weight,
    queries,
):
    z_at, y_at = lax.axis_index(Z), lax.axis_index("y")
    queries_all = lax.all_gather(queries, "y", axis=0, tiled=True)

    normed_patches = layer_norm(patches, patch_gain, patch_shift)
    enc_hidden = jax.nn.gelu(
        jnp.dot(normed_patches, encoder_up, preferred_element_type=F32), approximate=False
    ).astype(BF16)
    partial_out = jnp.dot(enc_hidden, encoder_down, preferred_element_type=F32).astype(BF16)
    share = tp_reduce_scatter(partial_out.reshape(4, 2, 16, -1))
    tp_at = lax.axis_index(TP)
    own_patches = pick(patches.reshape(8, 16, -1), tp_at)
    encoded = tp_all_gather((own_patches.astype(F32) + share).astype(BF16))
    encoded = encoded.reshape(patches.shape)

    rows, squares = project(hidden_text, norm_gain, kv_weight)
    packed = jnp.concatenate(
        [rows.reshape(8, TOK, TOK), jnp.broadcast_to(squares[None, None, :], (8, 8, TOK))], 1
    )
    summed = lax.psum_scatter(
        packed.reshape(-1, TOK), TP, scatter_dimension=0, tiled=True
    )
    inverse = lax.rsqrt(summed[TOK : TOK + 1] / D + 1e-05)
    sources = jnp.repeat(slot_source.astype(F32), IMG)[None, :]
    text_rows = jnp.concatenate(
        [summed[:TOK] * inverse, jnp.broadcast_to(sources, (ROWS - TOK, TOK))], 0
    ).astype(BF16)
    text_all = lax.all_gather(text_rows, Z, axis=0)

    image_emb = jnp.dot(encoded, proj_weight, preferred_element_type=F32).astype(BF16)
    rows, squares = project(image_emb, norm_gain, kv_weight)
    high = squares.astype(BF16)
    low = (squares - high.astype(F32)).astype(BF16)
    tail = jnp.concatenate(
        [high[None], low[None], jnp.zeros((ROWS - TOK - 2, IMG), BF16)], 0
    )
    packed = jnp.concatenate(
        [rows.astype(BF16).reshape(8, TOK, IMG), jnp.broadcast_to(tail[None], (8, *tail.shape))], 1
    )
    summed = tp_reduce_scatter(packed.reshape(4, 2, ROWS, IMG))
    inverse = lax.rsqrt((summed[TOK] + summed[TOK + 1])[None] / D + 1e-05)
    image_rows = (summed[:TOK] * inverse).astype(BF16)
    images_all = lax.all_to_all(
        jnp.broadcast_to(image_rows[None], (8, *image_rows.shape)), Z, 0, 0, tiled=True
    )

    frequencies = jnp.exp(
        jnp.arange(HALF, dtype=F32) * (-2.0 * math.log(500000.0) / (2 * HALF))
    )
    index = jnp.arange(8 * TOK, dtype=jnp.int32)
    positions = ((index // TOK) * 4 + y_at) * TOK + index % TOK
    angles = positions.astype(F32)[None, :] * frequencies[:, None]
    place = jnp.stack([z_at, y_at]).astype(jnp.int32)
    parts = attend(place, text_all, images_all, jnp.cos(angles), jnp.sin(angles), queries_all)
    received = [shift(parts[turn], "y", step) for turn, step in ((0, 2), (1, 3), (2, 0), (3, 1)) if step]
    return combine([parts[2], *received])


def solution(mesh):
    split = Mesh(mesh.devices.reshape(4, 2, 4, 4, 2), ("zh", "zl", "y", "x", "core"))
    seq = ("zh", "zl", "y")
    in_specs = (
        P(seq, None),
        P(),
        P(),
        P(None, TP),
        P(TP, None),
        P(None, TP),
        P(seq, TP),
        P(seq),
        P(TP),
        P(None, TP),
        P(seq, TP),
    )
    return jax.shard_map(
        body, mesh=split, in_specs=in_specs, out_specs=P(seq, TP), check_vma=False
    )
```

time: 384 us -> 178 us (0.46)
  waiting for transfers between devices: 281 us -> 51.3 us
  Pallas kernels: 0 us -> 49 us
  matrix products: 43.2 us -> 9.16 us
  starting transfers between devices: 0.35 us -> 21.9 us
  blocking collectives: 14.5 us -> 0 us
  local copies, waits for them, and re-layouts: 4.12 us -> 18.5 us
  other arithmetic: 23.6 us -> 11.7 us
    all_gather x3 -> x2, waiting for transfers between devices: 182 us -> 9.02 us  [the longest x1 9.02 us: body(): text_all = lax.all_gather(text_rows, Z, axis=0)]
    psum x1 -> x0, waiting for transfers between devices: 66.9 us -> none  [body(): summed_out = lax.psum(partial_out, 'tp')]
    pallas_call x0 -> x2, Pallas kernels: none -> 49 us  [the longest x1 46 us: attend(): pl.pallas_call(attend_kernel, out_shape=jax.ShapeDtypeStruct((4, ROWS, GR...]
    dot_general x5 -> x4, matrix products: 43.2 us -> 9.16 us  [the longest x2 5.15 us: project(): lax.dot_general(kv_weight, gained, (((1,), (1,)), ((), ())), preferred_el...]
    reduce_scatter x1, waiting for transfers between devices: 32.8 us -> 3.82 us  [body(): lax.psum_scatter(packed.reshape(-1, TOK), TP, scatter_dimension=0, tiled=...]
    ppermute x0 -> x15, waiting for transfers between devices: none -> 24.2 us  [shift(): lax.ppermute(values, axis, [(i, (i + step) % count) for i in range(count)])]
    ppermute x0 -> x15, starting transfers between devices: none -> 15.8 us  [shift(): lax.ppermute(values, axis, [(i, (i + step) % count) for i in range(count)])]
    reduce_sum x2 -> x1, other arithmetic: 16.2 us -> 1.37 us  [project(): squares = jnp.sum(jnp.square(widened), axis=1)]
  transfers between devices with their start and end apart: 5 -> 19, of which waited for: 5 -> 15; matrix products, arithmetic and copies ran while one was open for 0% -> 10% of each run, Pallas kernels for 0% -> 0%
where the time goes in v1:
time: 178 us; the launch traced here: 177 us
  waiting for transfers between devices  51.3 us (29%)
  Pallas kernels  49 us (28%)
  starting transfers between devices  21.9 us (12%)
  local copies, waits for them, and re-layouts  18.5 us (10%)
  between operations  15.2 us (9%)
  other arithmetic  11.7 us (7%)
  matrix products  9.16 us (5%)
    pallas_call x1, Pallas kernels, attend(): pl.pallas_call(attend_kernel, out_shape=jax.ShapeDtypeStruct((4, ROWS, GR...  46 us
    ppermute x15, waiting for transfers between devices, shift(): lax.ppermute(values, axis, [(i, (i + step) % count) for i in range(count)])  24.2 us
    ppermute x15, starting transfers between devices, shift(): lax.ppermute(values, axis, [(i, (i + step) % count) for i in range(count)])  15.8 us
    all_to_all x1, waiting for transfers between devices, body(): lax.all_to_all(jnp.broadcast_to(image_rows[None], (8, *image_rows.shape))...  14.2 us
    unnamed x35, local copies, waits for them, and re-layouts  9.69 us
    all_gather x1, waiting for transfers between devices, body(): text_all = lax.all_gather(text_rows, Z, axis=0)  9.02 us
    all_to_all x1, starting transfers between devices, body(): lax.all_to_all(jnp.broadcast_to(image_rows[None], (8, *image_rows.shape))...  6.02 us
    dot_general x2, matrix products, project(): lax.dot_general(kv_weight, gained, (((1,), (1,)), ((), ())), preferred_el...  5.15 us
  transfers between devices with their start and end apart: 19, of which 15 were waited for; matrix products, arithmetic and copies ran while one was open for 10% of the time, Pallas kernels for 0%

profile of v1, /device:TPU:224, one launch (start us, length us, event | category | flops | bytes accessed | tf_op | source)
XLA Modules:
  0.0 176.8 jit_solution(8959438724175839652)
XLA Ops:
  8.7 3.6 %fusion.10 = f32[256,2048]{1,0:T(8,128)S(1)} fusion(bf16[2048,1024]{1,0:T(8,128)(2,1)} %param.20, bf16[256,1024]{1,0:T(8,128)(2,1)} %param.17, f32[1024]{0:T(1024)} %param.19), kind=kOutput, calls=%fused_computation.23 | convolution fusion | flops 1074528256 | bytes 6819840 | tf_op jit(solution)/shard_map/dot_general | solution.py:74
  13.6 1.8 %pad_maximum_fusion = f32[8,264,256]{1,0,2:T(8,128)} fusion(f32[8,8,256]{1,0,2:T(8,128)S(1)} %broadcast_in_dim.29, f32[8,256,256]{1,0,2:T(8,128)S(1)} %bitcast.103), kind=kLoop, calls=%fused_computation | loop fusion | flops 540672 | bytes 4325376 | tf_op jit(solution)/shard_map/concatenate | solution.py:246
  15.5 3.4 %copy.22 = f32[8,264,256]{2,1,0:T(8,128)} copy(f32[8,264,256]{1,0,2:T(8,128)} %pad_maximum_fusion) | data formatting | bytes 4325376 | tf_op jit(solution)/shard_map/concatenate | solution.py:246
  20.2 3.4 %convolution_convert_fusion.1 = bf16[128,1280]{1,0:T(8,128)(2,1)S(1)} fusion(bf16[640,1280]{1,0:T(8,128)(2,1)} %param.15, bf16[1280,640]{1,0:T(8,128)(2,1)} %param.14, bf16[128,1280]{1,0:T(8,128)(2,1)S(1)} %copy-done.6, f32[1280]{0:T(1024)S(1)} %copy-done.14, f32[1280]{0:T(1024)S(1)} %copy-done.15, f32[128]{0:T(128)S(1)} %add_rsqrt_fusion, ...), kind=kOutput, calls=%fused_computation.2 | convolution fusion | flops 425902080 | bytes 3943424 | tf_op jit(solution)/shard_map/dot_general | solution.py:238
  27.0 2.8 %collective-permute-start.3 = (bf16[16,1280]{1,0:T(8,128)(2,1)}, bf16[16,1280]{1,0:T(8,128)(2,1)S(1)}, u32[]{:S(2)}, u32[]{:S(2)}) collective-permute-start(bf16[16,1280]{1,0:T(8,128)(2,1)} %get-tuple-element.21), channel_id=1, source_target_pairs={{0,6},{2,0},{4,2},{6,4},{1,7},{3,1},{5,3},{7,5},{8,14},{10,8},{12,... | collective-permute-start | bytes 122888 | tf_op jit(solution)/shard_map/ppermute | solution.py:30
  29.7 2.3 %collective-permute-start.1 = (bf16[16,1280]{1,0:T(8,128)(2,1)}, bf16[16,1280]{1,0:T(8,128)(2,1)S(1)}, u32[]{:S(2)}, u32[]{:S(2)}) collective-permute-start(bf16[16,1280]{1,0:T(8,128)(2,1)} %get-tuple-element.20), channel_id=1, source_target_pairs={{0,4},{2,6},{4,0},{6,2},{1,5},{3,7},{5,1},{7,3},{8,12},{10,14},{12... | collective-permute-start | bytes 122888 | tf_op jit(solution)/shard_map/ppermute | solution.py:30
  32.1 4.0 %collective-permute-done.2 = bf16[16,1280]{1,0:T(8,128)(2,1)S(1)} collective-permute-done((bf16[16,1280]{1,0:T(8,128)(2,1)}, bf16[16,1280]{1,0:T(8,128)(2,1)S(1)}, u32[]{:S(2)}, u32[]{:S(2)}) %collective-permute-start.2) | collective-permute-done | bytes 40992 | tf_op jit(solution)/shard_map/ppermute | solution.py:30
  37.6 1.8 %collective-permute-start.4 = (bf16[16,1280]{1,0:T(8,128)(2,1)S(1)}, bf16[16,1280]{1,0:T(8,128)(2,1)S(1)}, u32[]{:S(2)}, u32[]{:S(2)}) collective-permute-start(bf16[16,1280]{1,0:T(8,128)(2,1)S(1)} %get-tuple-element.8), channel_id=1, source_target_pairs={{0,4},{2,6},{4,0},{6,2},{1,5},{3,7},{5,1},{7,3},{8,12},{10,14},{12... | collective-permute-start | bytes 122888 | tf_op jit(solution)/shard_map/ppermute | solution.py:30
  39.5 1.8 %collective-permute-start.5 = (bf16[16,1280]{1,0:T(8,128)(2,1)S(1)}, bf16[16,1280]{1,0:T(8,128)(2,1)S(1)}, u32[]{:S(2)}, u32[]{:S(2)}) collective-permute-start(bf16[16,1280]{1,0:T(8,128)(2,1)S(1)} %get-tuple-element.8), channel_id=1, source_target_pairs={{0,2},{2,4},{4,6},{6,0},{1,3},{3,5},{5,7},{7,1},{8,10},{10,12},{12... | collective-permute-start | bytes 122888 | tf_op jit(solution)/shard_map/ppermute | solution.py:30
  43.4 1.6 collective-permute-done.5
  49.2 1.5 fusion
  54.4 3.8 %reduce-scatter.2.cloned.1.call-done = f32[264,256]{1,0:T(8,128)} async-done(((f32[2112,256]{1,0:T(8,128)}), f32[264,256]{1,0:T(8,128)}) %reduce-scatter.2.cloned.1.call-update) | async-done | bytes 270352 | tf_op jit(solution)/shard_map/reduce_scatter | solution.py:249
  60.8 2.0 %collective-permute-start.10 = (bf16[272,128]{1,0:T(8,128)(2,1)S(1)}, bf16[272,128]{1,0:T(8,128)(2,1)S(1)}, u32[]{:S(2)}, u32[]{:S(2)}) collective-permute-start(bf16[272,128]{1,0:T(8,128)(2,1)S(1)} %get-tuple-element.19), channel_id=1, source_target_pairs={{0,2},{2,4},{4,6},{6,0},{1,3},{3,5},{5,7},{7,1},{8,10},{10,12},{12... | collective-permute-start | bytes 208904 | tf_op jit(solution)/shard_map/ppermute | solution.py:30
  62.8 2.3 %collective-permute-done.11 = bf16[272,128]{1,0:T(8,128)(2,1)S(1)} collective-permute-done((bf16[272,128]{1,0:T(8,128)(2,1)S(1)}, bf16[272,128]{1,0:T(8,128)(2,1)S(1)}, u32[]{:S(2)}, u32[]{:S(2)}) %collective-permute-start.11) | collective-permute-done | bytes 69664 | tf_op jit(solution)/shard_map/ppermute | solution.py:30
  65.1 2.3 %collective-permute-done.10 = bf16[272,128]{1,0:T(8,128)(2,1)S(1)} collective-permute-done((bf16[272,128]{1,0:T(8,128)(2,1)S(1)}, bf16[272,128]{1,0:T(8,128)(2,1)S(1)}, u32[]{:S(2)}, u32[]{:S(2)}) %collective-permute-start.10) | collective-permute-done | bytes 69664 | tf_op jit(solution)/shard_map/ppermute | solution.py:30
  69.6 6.0 %all-to-all-start = ((bf16[8,256,128]{2,1,0:T(8,128)(2,1)}), bf16[8,256,128]{2,1,0:T(8,128)(2,1)S(1)}, u32[]{:S(2)}, u32[]{:S(2)}) async-start(bf16[8,256,128]{2,1,0:T(8,128)(2,1)} %broadcast_in_dim.69), calls=%async_computation.1 | async-start | bytes 1048576 | tf_op jit(solution)/shard_map/all_to_all | solution.py:272
  75.7 2.8 %multiply_sine_fusion = (f32[64,2048]{1,0:T(8,128)}, f32[64,2048]{1,0:T(8,128)}) fusion(f32[64]{0:T(128)S(1)} %multiply_exponential_fusion, f32[2048]{0:T(1024)S(1)} %fusion.86), kind=kLoop, calls=%fused_computation.16 | loop fusion | flops 131072 | bytes 1057024 | tf_op jit(solution)/shard_map/sin | solution.py:283
  78.5 14.2 %all-to-all-done.image_ref = bf16[8,256,128]{2,1,0:T(8,128)(2,1)S(1)} async-done(((bf16[8,256,128]{2,1,0:T(8,128)(2,1)}), bf16[8,256,128]{2,1,0:T(8,128)(2,1)S(1)}, u32[]{:S(2)}, u32[]{:S(2)}) %all-to-all-start) | async-done | bytes 524320 | tf_op jit(solution)/shard_map/all_to_all | solution.py:272
  92.7 9.0 %all-gather.3.cloned.1.call-done.text_ref = bf16[8,272,256]{2,1,0:T(8,128)(2,1)} async-done(((bf16[1,272,256]{2,1,0:T(8,128)(2,1)}), bf16[8,272,256]{2,1,0:T(8,128)(2,1)}) %all-gather.3.cloned.1.call-update) | async-done | bytes 1114128 | tf_op jit(solution)/shard_map/all_gather | solution.py:257
  106.3 46.0 %attend.1 = bf16[4,272,512]{2,1,0:T(8,128)(2,1)S(1)} custom-call(s32[2]{0:T(128)S(1)} %pad_add_fusion.place, bf16[8,272,256]{2,1,0:T(8,128)(2,1)S(1)} %copy-done.3, bf16[8,256,128]{2,1,0:T(8,128)(2,1)S(1)} %all-to-all-done.image_ref, f32[64,2048]{1,0:T(8,128)S(1)} %copy-done.2, f32[64,2048]{1,0:T(8,128)S(1)} %copy-done.1, bf16[1024,512]{1,0:T(8,128)(2,1)S(1)} %copy-done.4), custom_call_target="tpu_custom_call" | custom-call | tf_op jit(solution)/shard_map/attend/pallas_call | solution.py:165
  153.8 2.5 %collective-permute-start.13 = (bf16[272,512]{1,0:T(8,128)(2,1)S(1)}, bf16[272,512]{1,0:T(8,128)(2,1)S(1)}, u32[]{:S(2)}, u32[]{:S(2)}) collective-permute-start(bf16[272,512]{1,0:T(8,128)(2,1)S(1)} %get-tuple-element.12), channel_id=1, source_target_pairs={{0,24},{8,0},{16,8},{24,16},{1,25},{9,1},{17,9},{25,17},{2,26},{10... | collective-permute-start | bytes 835592 | tf_op jit(solution)/shard_map/ppermute | solution.py:30
  156.3 6.5 %collective-permute-done.12.refs_1_ = bf16[272,512]{1,0:T(8,128)(2,1)S(1)} collective-permute-done((bf16[272,512]{1,0:T(8,128)(2,1)S(1)}, bf16[272,512]{1,0:T(8,128)(2,1)S(1)}, u32[]{:S(2)}, u32[]{:S(2)}) %collective-permute-start.12) | collective-permute-done | bytes 278560 | tf_op jit(solution)/shard_map/ppermute | solution.py:30
  163.0 2.6 %collective-permute-done.14.refs_3_ = bf16[272,512]{1,0:T(8,128)(2,1)S(1)} collective-permute-done((bf16[272,512]{1,0:T(8,128)(2,1)S(1)}, bf16[272,512]{1,0:T(8,128)(2,1)S(1)}, u32[]{:S(2)}, u32[]{:S(2)}) %collective-permute-start.14) | collective-permute-done | bytes 278560 | tf_op jit(solution)/shard_map/ppermute | solution.py:30
  166.4 3.0 %combine.1 = bf16[256,512]{1,0:T(8,128)(2,1)} custom-call(bf16[272,512]{1,0:T(8,128)(2,1)} %get-tuple-element.14.refs_0_, bf16[272,512]{1,0:T(8,128)(2,1)} %copy-done.8, bf16[272,512]{1,0:T(8,128)(2,1)} %copy-done.9, bf16[272,512]{1,0:T(8,128)(2,1)} %copy-done.10), custom_call_target="tpu_custom_call" | custom-call | tf_op jit(solution)/shard_map/combine/pallas_call | solution.py:211
  (102 shorter events, 30.6 us)
Async XLA Ops:
  7.4 39.8 %copy-start = (bf16[1280,1024]{1,0:T(8,128)(2,1)S(1)}, bf16[1280,1024]{1,0:T(8,128)(2,1)}, u32[]{:S(2)}) copy-start(bf16[1280,1024]{1,0:T(8,128)(2,1)} %param.16) | copy-start | bytes 7864324
  7.4 50.8 %reduce-scatter.2.cloned.1.call-start = ((), (), s32[]{:S(2)}) async-start(), calls=%async_computation.2 | async-start | bytes 2433024 | tf_op jit(solution)/shard_map/reduce_scatter | solution.py:249
  18.9 59.6 %all-gather.5.cloned.1.call-start = ((), (), s32[]{:S(2)}) async-start(), calls=%async_computation.4 | async-start | bytes 1310720 | tf_op jit(solution)/shard_map/all_gather | solution.py:232
  23.6 15.8 %copy-start.16 = (s32[2]{0:T(128)S(1)}, s32[2]{0:T(128)}, u32[]{:S(2)}) copy-start(s32[2]{0:T(128)} %param.18) | copy-start | bytes 28
  23.7 1.6 collective-permute-start
  27.0 5.1 %collective-permute-start.3 = (bf16[16,1280]{1,0:T(8,128)(2,1)}, bf16[16,1280]{1,0:T(8,128)(2,1)S(1)}, u32[]{:S(2)}, u32[]{:S(2)}) collective-permute-start(bf16[16,1280]{1,0:T(8,128)(2,1)} %get-tuple-element.21), channel_id=1, source_target_pairs={{0,6},{2,0},{4,2},{6,4},{1,7},{3,1},{5,3},{7,5},{8,14},{10,8},{12,... | collective-permute-start | bytes 122888 | tf_op jit(solution)/shard_map/ppermute | solution.py:30
  29.7 6.4 %collective-permute-start.2 = (bf16[16,1280]{1,0:T(8,128)(2,1)}, bf16[16,1280]{1,0:T(8,128)(2,1)S(1)}, u32[]{:S(2)}, u32[]{:S(2)}) collective-permute-start(bf16[16,1280]{1,0:T(8,128)(2,1)} %get-tuple-element.22), channel_id=1, source_target_pairs={{0,2},{2,4},{4,6},{6,0},{1,3},{3,5},{5,7},{7,1},{8,10},{10,12},{12... | collective-permute-start | bytes 122888 | tf_op jit(solution)/shard_map/ppermute | solution.py:30
  29.7 6.4 %collective-permute-start.1 = (bf16[16,1280]{1,0:T(8,128)(2,1)}, bf16[16,1280]{1,0:T(8,128)(2,1)S(1)}, u32[]{:S(2)}, u32[]{:S(2)}) collective-permute-start(bf16[16,1280]{1,0:T(8,128)(2,1)} %get-tuple-element.20), channel_id=1, source_target_pairs={{0,4},{2,6},{4,0},{6,2},{1,5},{3,7},{5,1},{7,3},{8,12},{10,14},{12... | collective-permute-start | bytes 122888 | tf_op jit(solution)/shard_map/ppermute | solution.py:30
  32.1 69.7 %all-gather.3.cloned.1.call-start = ((), (), s32[]{:S(2)}) async-start(), calls=%async_computation.3 | async-start | bytes 1253376 | tf_op jit(solution)/shard_map/all_gather | solution.py:257
  37.6 5.8 %collective-permute-start.4 = (bf16[16,1280]{1,0:T(8,128)(2,1)S(1)}, bf16[16,1280]{1,0:T(8,128)(2,1)S(1)}, u32[]{:S(2)}, u32[]{:S(2)}) collective-permute-start(bf16[16,1280]{1,0:T(8,128)(2,1)S(1)} %get-tuple-element.8), channel_id=1, source_target_pairs={{0,4},{2,6},{4,0},{6,2},{1,5},{3,7},{5,1},{7,3},{8,12},{10,14},{12... | collective-permute-start | bytes 122888 | tf_op jit(solution)/shard_map/ppermute | solution.py:30
  39.5 5.4 %collective-permute-start.5 = (bf16[16,1280]{1,0:T(8,128)(2,1)S(1)}, bf16[16,1280]{1,0:T(8,128)(2,1)S(1)}, u32[]{:S(2)}, u32[]{:S(2)}) collective-permute-start(bf16[16,1280]{1,0:T(8,128)(2,1)S(1)} %get-tuple-element.8), channel_id=1, source_target_pairs={{0,2},{2,4},{4,6},{6,0},{1,3},{3,5},{5,7},{7,1},{8,10},{10,12},{12... | collective-permute-start | bytes 122888 | tf_op jit(solution)/shard_map/ppermute | solution.py:30
  41.3 4.3 %collective-permute-start.6 = (bf16[16,1280]{1,0:T(8,128)(2,1)S(1)}, bf16[16,1280]{1,0:T(8,128)(2,1)S(1)}, u32[]{:S(2)}, u32[]{:S(2)}) collective-permute-start(bf16[16,1280]{1,0:T(8,128)(2,1)S(1)} %get-tuple-element.8), channel_id=1, source_target_pairs={{0,6},{2,0},{4,2},{6,4},{1,7},{3,1},{5,3},{7,5},{8,14},{10,8},{12,... | collective-permute-start | bytes 122888 | tf_op jit(solution)/shard_map/ppermute | solution.py:30
  45.6 1.4 collective-permute-start.7
  47.0 2.2 %copy-start.5 = (bf16[2048,1024]{1,0:T(8,128)(2,1)S(1)}, bf16[2048,1024]{1,0:T(8,128)(2,1)}, u32[]{:S(2)}) copy-start(bf16[2048,1024]{1,0:T(8,128)(2,1)} %param.20) | copy-start | bytes 12582916
  54.1 6.4 %collective-permute-start.8 = (bf16[4,272,128]{2,1,0:T(8,128)(2,1)}, bf16[4,272,128]{2,1,0:T(8,128)(2,1)S(1)}, u32[]{:S(2)}, u32[]{:S(2)}) collective-permute-start(bf16[4,272,128]{2,1,0:T(8,128)(2,1)} %fusion.34), channel_id=1, source_target_pairs={{0,1},{1,0},{2,3},{3,2},{4,5},{5,4},{6,7},{7,6},{8,9},{9,8},{10,11... | collective-permute-start | bytes 835592 | tf_op jit(solution)/shard_map/ppermute | solution.py:30
  60.7 4.4 %collective-permute-start.11 = (bf16[272,128]{1,0:T(8,128)(2,1)S(1)}, bf16[272,128]{1,0:T(8,128)(2,1)S(1)}, u32[]{:S(2)}, u32[]{:S(2)}) collective-permute-start(bf16[272,128]{1,0:T(8,128)(2,1)S(1)} %get-tuple-element.18), channel_id=1, source_target_pairs={{0,6},{2,0},{4,2},{6,4},{1,7},{3,1},{5,3},{7,5},{8,14},{10,8},{12,... | collective-permute-start | bytes 208904 | tf_op jit(solution)/shard_map/ppermute | solution.py:30
  60.8 6.6 %collective-permute-start.10 = (bf16[272,128]{1,0:T(8,128)(2,1)S(1)}, bf16[272,128]{1,0:T(8,128)(2,1)S(1)}, u32[]{:S(2)}, u32[]{:S(2)}) collective-permute-start(bf16[272,128]{1,0:T(8,128)(2,1)S(1)} %get-tuple-element.19), channel_id=1, source_target_pairs={{0,2},{2,4},{4,6},{6,0},{1,3},{3,5},{5,7},{7,1},{8,10},{10,12},{12... | collective-permute-start | bytes 208904 | tf_op jit(solution)/shard_map/ppermute | solution.py:30
  62.8 5.8 %collective-permute-start.9 = (bf16[272,128]{1,0:T(8,128)(2,1)S(1)}, bf16[272,128]{1,0:T(8,128)(2,1)S(1)}, u32[]{:S(2)}, u32[]{:S(2)}) collective-permute-start(bf16[272,128]{1,0:T(8,128)(2,1)S(1)} %get-tuple-element.17), channel_id=1, source_target_pairs={{0,4},{2,6},{4,0},{6,2},{1,5},{3,7},{5,1},{7,3},{8,12},{10,14},{12... | collective-permute-start | bytes 208904 | tf_op jit(solution)/shard_map/ppermute | solution.py:30
  69.6 23.1 %all-to-all-start = ((bf16[8,256,128]{2,1,0:T(8,128)(2,1)}), bf16[8,256,128]{2,1,0:T(8,128)(2,1)S(1)}, u32[]{:S(2)}, u32[]{:S(2)}) async-start(bf16[8,256,128]{2,1,0:T(8,128)(2,1)} %broadcast_in_dim.69), calls=%async_computation.1 | async-start | bytes 1048576 | tf_op jit(solution)/shard_map/all_to_all | solution.py:272
  153.1 9.7 %collective-permute-start.12 = (bf16[272,512]{1,0:T(8,128)(2,1)S(1)}, bf16[272,512]{1,0:T(8,128)(2,1)S(1)}, u32[]{:S(2)}, u32[]{:S(2)}) collective-permute-start(bf16[272,512]{1,0:T(8,128)(2,1)S(1)} %get-tuple-element.13), channel_id=1, source_target_pairs={{0,16},{8,24},{16,0},{24,8},{1,17},{9,25},{17,1},{25,9},{2,18},{10... | collective-permute-start | bytes 835592 | tf_op jit(solution)/shard_map/ppermute | solution.py:30
  153.8 9.2 %collective-permute-start.13 = (bf16[272,512]{1,0:T(8,128)(2,1)S(1)}, bf16[272,512]{1,0:T(8,128)(2,1)S(1)}, u32[]{:S(2)}, u32[]{:S(2)}) collective-permute-start(bf16[272,512]{1,0:T(8,128)(2,1)S(1)} %get-tuple-element.12), channel_id=1, source_target_pairs={{0,24},{8,0},{16,8},{24,16},{1,25},{9,1},{17,9},{25,17},{2,26},{10... | collective-permute-start | bytes 835592 | tf_op jit(solution)/shard_map/ppermute | solution.py:30
  156.3 9.3 %collective-permute-start.14 = (bf16[272,512]{1,0:T(8,128)(2,1)S(1)}, bf16[272,512]{1,0:T(8,128)(2,1)S(1)}, u32[]{:S(2)}, u32[]{:S(2)}) collective-permute-start(bf16[272,512]{1,0:T(8,128)(2,1)S(1)} %get-tuple-element.11), channel_id=1, source_target_pairs={{0,8},{8,16},{16,24},{24,0},{1,9},{9,17},{17,25},{25,1},{2,10},{10... | collective-permute-start | bytes 835592 | tf_op jit(solution)/shard_map/ppermute | solution.py:30
  162.8 2.9 %copy-start.8 = (bf16[272,512]{1,0:T(8,128)(2,1)}, bf16[272,512]{1,0:T(8,128)(2,1)S(1)}, u32[]{:S(2)}) copy-start(bf16[272,512]{1,0:T(8,128)(2,1)S(1)} %collective-permute-done.12.refs_1_) | copy-start | bytes 835588
  163.0 2.6 %copy-start.9 = (bf16[272,512]{1,0:T(8,128)(2,1)}, bf16[272,512]{1,0:T(8,128)(2,1)S(1)}, u32[]{:S(2)}) copy-start(bf16[272,512]{1,0:T(8,128)(2,1)S(1)} %collective-permute-done.13.refs_2_) | copy-start | bytes 835588
  (12 other events, 13.1 us)
Sparse Core Ops, SparseCore 0:
  19.0 39.1 reduce-scatter.1
Sparse Core Ops, SparseCore 1:
  32.1 25.9 all-gather.4
  60.7 41.0 all-gather.2

commit v2 on v1

v2 whole, which is shorter than its diff:
```python
import functools
import math

import jax
import jax.numpy as jnp
from jax import lax
from jax.experimental import pallas as pl
from jax.experimental.pallas import tpu as pltpu
from jax.sharding import Mesh
from jax.sharding import PartitionSpec as P

D = 8192
HEAD = 128
HALF = 64
GROUP = 4
TOK = 256
IMG = 128
ROWS = 272
TP = ("x", "core")
Z = ("zh", "zl")
BF16 = jnp.bfloat16
F32 = jnp.float32
NEG = -1e30
LOG2E = math.log2(math.e)
KEYS = 2048
CHUNK = 512
ROWS_Q = GROUP * TOK
SCALE = HEAD ** (-0.5)


def shift(values, axis, step):
    count = lax.axis_size(axis)
    return lax.ppermute(values, axis, [(i, (i + step) % count) for i in range(count)])


def pick(values, index):
    return lax.dynamic_index_in_dim(values, index, 0, keepdims=False)


def vmem(mib):
    return pltpu.CompilerParams(vmem_limit_bytes=mib * 1024 * 1024)


def split_squares(column, count):
    row = jnp.broadcast_to(column, (count, HEAD)).T[:16]
    high = row.astype(BF16).astype(F32)
    at = lax.broadcasted_iota(jnp.int32, row.shape, 0)
    return jnp.where(at == 0, high, jnp.where(at == 1, row - high, 0.0)).astype(BF16)


def head_rows(step, features, tail, weight_ref, give_ref, keep_ref):
    rows = lax.dot_general(
        weight_ref[...], features[...], (((1,), (1,)), ((), ())), preferred_element_type=F32
    ).astype(BF16)

    @pl.when(step < 4)
    def to_other_core():
        give_ref[0, :TOK, :] = rows
        give_ref[0, TOK:, :] = tail[...]

    @pl.when(step >= 4)
    def own_core():
        keep_ref[0, :TOK, :] = rows
        keep_ref[0, TOK:, :] = tail[...]


def gain_features(features, gain_ref, gained, tail):
    widened = features.astype(F32)
    squares = jnp.sum(jnp.square(widened), axis=1, keepdims=True)
    tail[...] = split_squares(squares, features.shape[0])
    gained[...] = (widened * gain_ref[...]).astype(BF16)


def text_project_kernel(core, hidden_ref, gain_ref, weight_ref, give_ref, keep_ref, gained, tail):
    step = pl.program_id(0)

    @pl.when(step == 0)
    def first():
        gain_features(hidden_ref[...], gain_ref, gained, tail)

    head_rows(step, gained, tail, weight_ref, give_ref, keep_ref)


def image_project_kernel(
    core, half_ref, other_ref, proj_ref, gain_ref, weight_ref, give_ref, keep_ref, encoded, gained, tail
):
    step = pl.program_id(0)

    @pl.when(step == 0)
    def first():
        @pl.when(core[0] == 0)
        def low():
            encoded[:HALF, :] = half_ref[...]
            encoded[HALF:, :] = other_ref[...]

        @pl.when(core[0] == 1)
        def high():
            encoded[:HALF, :] = other_ref[...]
            encoded[HALF:, :] = half_ref[...]

        image = jnp.dot(encoded[...], proj_ref[...], preferred_element_type=F32).astype(BF16)
        gain_features(image, gain_ref, gained, tail)

    head_rows(step, gained, tail, weight_ref, give_ref, keep_ref)


def project(kernel, features, norm_gain, kv_weight, core, count, scratch):
    whole = lambda step, core: (0, 0)
    mine = jnp.reshape(core, (1,)).astype(jnp.int32)

    def head(step, core):
        x_at = jnp.where(step < 4, step, step - 4)
        return (2 * x_at + jnp.where(step < 4, 1 - core[0], core[0]), 0)

    shape = jax.ShapeDtypeStruct((4, ROWS, count), BF16)
    return pl.pallas_call(
        kernel,
        out_shape=(shape, shape),
        grid_spec=pltpu.PrefetchScalarGridSpec(
            num_scalar_prefetch=1,
            grid=(8,),
            in_specs=[
                *[pl.BlockSpec(f.shape, whole) for f in features],
                pl.BlockSpec((1, norm_gain.shape[0]), whole),
                pl.BlockSpec((TOK, kv_weight.shape[1]), head),
            ],
            out_specs=(
                pl.BlockSpec((1, ROWS, count), lambda step, core: (jnp.minimum(step, 3), 0, 0)),
                pl.BlockSpec((1, ROWS, count), lambda step, core: (jnp.maximum(step, 4) - 4, 0, 0)),
            ),
            scratch_shapes=[
                *scratch,
                pltpu.VMEM((count, kv_weight.shape[1]), BF16),
                pltpu.VMEM((16, count), BF16),
            ],
        ),
        compiler_params=vmem(24),
    )(mine, *features, norm_gain[None, :], kv_weight)


def pair_kernel(place, keep_ref, got_ref, own_ref, two_ref, one_ref, three_ref):
    for step, ref in ((2, two_ref), (1, one_ref), (3, three_ref), (0, own_ref)):
        at = lax.rem(place[0] + step, 4)
        total = keep_ref[at].astype(F32) + got_ref[at].astype(F32)
        ref[...] = total.astype(ref.dtype)


def add_pair(keep, got, x_at):
    part = keep.shape[1:]
    return pl.pallas_call(
        pair_kernel,
        out_shape=(jax.ShapeDtypeStruct(part, F32), *[jax.ShapeDtypeStruct(part, BF16)] * 3),
        in_specs=[
            pl.BlockSpec(memory_space=pltpu.SMEM),
            *[pl.BlockSpec(memory_space=pltpu.VMEM)] * 2,
        ],
        name="add_pair",
    )(jnp.reshape(x_at, (1,)).astype(jnp.int32), keep, got)


def finish_kernel(slots, *refs):
    *inputs, out_ref = refs
    total = inputs[0][...]
    for ref in inputs[1:]:
        total = total + ref[...].astype(F32)
    inverse = lax.rsqrt((total[TOK : TOK + 1] + total[TOK + 1 : TOK + 2]) / D + 1e-05)
    rows = (total[:TOK] * inverse).astype(BF16)
    for copy in range(8):
        out_ref[copy, :TOK, :] = rows
    if out_ref.shape[1] > TOK:
        lane = lax.broadcasted_iota(jnp.int32, (ROWS - TOK, out_ref.shape[2]), 1)
        source = jnp.where(lane < IMG, slots[0], slots[1]).astype(F32).astype(BF16)
        for copy in range(8):
            out_ref[copy, TOK:, :] = source


def finish_rows(slots, pieces, row_count):
    count = pieces[0].shape[1]
    return pl.pallas_call(
        finish_kernel,
        out_shape=jax.ShapeDtypeStruct((8, row_count, count), BF16),
        in_specs=[
            pl.BlockSpec(memory_space=pltpu.SMEM),
            *[pl.BlockSpec(memory_space=pltpu.VMEM)] * 4,
        ],
        name="finish_rows",
    )(slots, *pieces)


def scatter_rows(give, keep, slots, x_at, row_count):
    got = shift(give, "core", 1)
    own, two, one, three = add_pair(keep, got, x_at)
    pieces = [own, shift(two, "x", 2), shift(one, "x", 1), shift(three, "x", 3)]
    return finish_rows(slots, pieces, row_count)


def merge_kernel(text_ref, image_ref, cos_ref, sin_ref, keys, values):
    values[:, HEAD:] = jnp.ones((KEYS, HEAD), BF16)
    for block in range(8):
        for slot in range(2):
            lanes = slice(slot * IMG, (slot + 1) * IMG)
            here = slice(block * TOK + slot * IMG, block * TOK + (slot + 1) * IMG)
            text = text_ref[block, :, lanes].astype(F32)
            source = text[TOK : TOK + 1, :]
            rows = text[:TOK, :]
            for r in range(4):
                rows = jnp.where(
                    source == float(r), image_ref[2 * r + block % 2].astype(F32), rows
                )
            cosine, sine = cos_ref[:, here], sin_ref[:, here]
            first, second = rows[:HALF], rows[HALF:HEAD]
            keys[:HALF, here] = (first * cosine - second * sine).astype(BF16)
            keys[HALF:, here] = (second * cosine + first * sine).astype(BF16)
            values[here, :HEAD] = rows[HEAD:].T.astype(BF16)


def merge(text, images, cosine, sine):
    return pl.pallas_call(
        merge_kernel,
        out_shape=(
            jax.ShapeDtypeStruct((HEAD, KEYS), BF16),
            jax.ShapeDtypeStruct((KEYS, 2 * HEAD), BF16),
        ),
        compiler_params=vmem(24),
        name="merge",
    )(text, images, cosine, sine)


def attend_kernel(step, place, keys, values, query_ref, out_ref, stacked, scores, top, mixed):
    z_at, y_at = place[0], place[1]
    block_at = lax.rem(y_at + step, 4)
    for h in range(GROUP):
        stacked[h * TOK : (h + 1) * TOK, :] = query_ref[:, h * HEAD : (h + 1) * HEAD]
    full = z_at + jnp.where(y_at < block_at, 1, 0)
    count = z_at + jnp.where(y_at <= block_at, 1, 0)
    plain = full // 2
    chunks = (count + 1) // 2
    top[...] = jnp.full(top.shape, NEG, F32)
    mixed[...] = jnp.zeros(mixed.shape, F32)

    def chunk_at(chunk):
        return pl.ds(pl.multiple_of(chunk * CHUNK, CHUNK), CHUNK)

    def score(chunk, masked):
        at = chunk_at(chunk)
        keys_now = keys[:, at]
        if masked:
            key_at = lax.broadcasted_iota(jnp.int32, (TOK, CHUNK), 1)
            low = jnp.where(key_at < TOK, key_at, key_at - TOK + 4 * TOK)
            query_at = lax.broadcasted_iota(jnp.int32, (TOK, CHUNK), 0)
            offset = ((2 * chunk - z_at) * 4 + y_at - block_at) * TOK
            allowed = low + offset <= query_at
        for h in range(GROUP):
            here = slice(h * TOK, (h + 1) * TOK)
            s = jnp.dot(stacked[here, :], keys_now, preferred_element_type=F32)
            if masked:
                s = jnp.where(allowed, s, -jnp.inf)
            scores[here, at] = s
            most = top[here, :]
            for lane in range(0, CHUNK, HEAD):
                most = jnp.maximum(most, s[:, lane : lane + HEAD])
            top[here, :] = most

    pl.loop(0, plain)(lambda chunk: score(chunk, False))

    @pl.when(chunks > plain)
    def last():
        score(plain, True)

    offset = jnp.max(top[...], axis=1, keepdims=True) * (SCALE * LOG2E)
    top[...] = jnp.broadcast_to(offset, top.shape)

    @pl.loop(0, chunks)
    def weigh(chunk):
        at = chunk_at(chunk)
        values_now = values[at, :]
        for h in range(GROUP):
            here = slice(h * TOK, (h + 1) * TOK)
            weights = jnp.exp2(scores[here, at] * (SCALE * LOG2E) - top[here, :1]).astype(BF16)
            mixed[here, :] += jnp.dot(weights, values_now, preferred_element_type=F32)

    lane = lax.broadcasted_iota(jnp.int32, (TOK, HEAD), 1)
    stats = jnp.zeros((TOK, HEAD), F32)
    for h in range(GROUP):
        here = slice(h * TOK, (h + 1) * TOK)
        total = mixed[here, HEAD:]
        some = total > 0.0
        safe = jnp.where(some, total, 1.0)
        out_ref[:TOK, h * HEAD : (h + 1) * HEAD] = (mixed[here, :HEAD] / safe).astype(BF16)
        level = jnp.where(some, top[here, :] + jnp.log2(safe), NEG)
        for part in range(3):
            piece = level.astype(BF16).astype(F32)
            stats = jnp.where(lane == 3 * h + part, piece, stats)
            level = level - piece
    out_ref[TOK:, :TOK] = stats.T[: ROWS - TOK].astype(BF16)
    out_ref[TOK:, TOK:] = jnp.zeros((ROWS - TOK, 2 * HEAD), BF16)


def attend(step, place, keys, values, queries):
    return pl.pallas_call(
        functools.partial(attend_kernel, step),
        out_shape=jax.ShapeDtypeStruct((ROWS, GROUP * HEAD), BF16),
        in_specs=[
            pl.BlockSpec(memory_space=pltpu.SMEM),
            *[pl.BlockSpec(memory_space=pltpu.VMEM)] * 3,
        ],
        scratch_shapes=[
            pltpu.VMEM((ROWS_Q, HEAD), BF16),
            pltpu.VMEM((ROWS_Q, KEYS), F32),
            pltpu.VMEM((ROWS_Q, HEAD), F32),
            pltpu.VMEM((ROWS_Q, 2 * HEAD), F32),
        ],
        compiler_params=vmem(40),
        cost_estimate=pl.CostEstimate(
            flops=4 * ROWS_Q * KEYS * HEAD, bytes_accessed=2 << 20, transcendentals=ROWS_Q * KEYS
        ),
        name="attend",
    )(place, keys, values, queries)


def layer_norm(values, norm_scale, norm_shift):
    widened = values.astype(F32)
    center = jnp.mean(widened, axis=-1, keepdims=True)
    spread = jnp.mean(jnp.square(widened - center), axis=-1, keepdims=True)
    return ((widened - center) * lax.rsqrt(spread + 1e-06) * norm_scale + norm_shift).astype(BF16)


def combine_kernel(*refs):
    out_ref = refs[-1]
    levels = []
    for ref in refs[:-1]:
        rows = ref[TOK:, :TOK].astype(F32)
        levels.append(jnp.concatenate([rows, jnp.zeros((HEAD - rows.shape[0], TOK), F32)], 0).T)
    for h in range(GROUP):
        lanes = slice(h * HEAD, (h + 1) * HEAD)
        level = [
            l[:, 3 * h : 3 * h + 1] + l[:, 3 * h + 1 : 3 * h + 2] + l[:, 3 * h + 2 : 3 * h + 3]
            for l in levels
        ]
        most = functools.reduce(jnp.maximum, level)
        weights = [jnp.exp2(l - most) for l in level]
        total = sum(weights)
        mixed = sum(w * ref[:TOK, lanes].astype(F32) for w, ref in zip(weights, refs[:-1]))
        out_ref[:, lanes] = (mixed / total).astype(BF16)


def combine(parts):
    return pl.pallas_call(
        combine_kernel,
        out_shape=jax.ShapeDtypeStruct((TOK, GROUP * HEAD), BF16),
        name="combine",
    )(*parts)


def body(
    patches,
    patch_gain,
    patch_shift,
    encoder_up,
    encoder_down,
    proj_weight,
    hidden_text,
    slot_source,
    norm_gain,
    kv_weight,
    queries,
):
    z_at, y_at = lax.axis_index(Z), lax.axis_index("y")
    x_at, core = lax.axis_index("x"), lax.axis_index("core")

    give, keep = project(text_project_kernel, [hidden_text], norm_gain, kv_weight, core, TOK, [])
    text_rows = scatter_rows(give, keep, slot_source, x_at, ROWS)
    text_all = lax.all_to_all(text_rows, Z, 0, 0, tiled=True)

    normed_patches = layer_norm(patches, patch_gain, patch_shift)
    enc_hidden = jax.nn.gelu(
        jnp.dot(normed_patches, encoder_up, preferred_element_type=F32), approximate=False
    ).astype(BF16)
    partial_out = jnp.dot(enc_hidden, encoder_down, preferred_element_type=F32).astype(BF16)
    halves = partial_out.reshape(2, HALF, -1)
    half = pick(halves, core).astype(F32) + shift(pick(halves, 1 - core), "core", 1).astype(F32)
    sent = half.astype(BF16)
    for step in (2, 1, 3):
        half = half + shift(sent, "x", step).astype(F32)
    half = (half + pick(patches.reshape(2, HALF, -1), core).astype(F32)).astype(BF16)
    other = shift(half, "core", 1)

    give, keep = project(
        image_project_kernel,
        [half, other, proj_weight],
        norm_gain,
        kv_weight,
        core,
        IMG,
        [pltpu.VMEM(patches.shape, BF16)],
    )
    image_rows = scatter_rows(give, keep, slot_source, x_at, TOK)
    images_all = lax.all_to_all(image_rows, Z, 0, 0, tiled=True)

    frequencies = jnp.exp(
        jnp.arange(HALF, dtype=F32) * (-2.0 * math.log(500000.0) / (2 * HALF))
    )
    index = jnp.arange(KEYS, dtype=jnp.int32)
    positions = ((index // TOK) * 4 + y_at) * TOK + index % TOK
    angles = positions.astype(F32)[None, :] * frequencies[:, None]
    keys, values = merge(text_all, images_all, jnp.cos(angles), jnp.sin(angles))
    place = jnp.stack([z_at, y_at]).astype(jnp.int32)
    received = []
    for step in (2, 1, 3):
        asked = shift(queries, "y", 4 - step)
        received.append(shift(attend(step, place, keys, values, asked), "y", step))
    return combine([attend(0, place, keys, values, queries), *received])


def solution(mesh):
    split = Mesh(mesh.devices.reshape(4, 2, 4, 4, 2), ("zh", "zl", "y", "x", "core"))
    seq = ("zh", "zl", "y")
    in_specs = (
        P(seq, None),
        P(),
        P(),
        P(None, TP),
        P(TP, None),
        P(None, TP),
        P(seq, TP),
        P(seq),
        P(TP),
        P(None, TP),
        P(seq, TP),
    )
    return jax.shard_map(
        body, mesh=split, in_specs=in_specs, out_specs=P(seq, TP), check_vma=False
    )
```

time: 178 us -> 144 us (0.81)
  starting transfers between devices: 21.9 us -> 38.5 us
  between operations: 15.2 us -> 0.21 us
  waiting for transfers between devices: 51.3 us -> 41.6 us
  Pallas kernels: 49 us -> 40.4 us
  other arithmetic: 11.7 us -> 5.54 us
  matrix products: 9.16 us -> 3.08 us
  local copies, waits for them, and re-layouts: 18.5 us -> 14.2 us
    ppermute x15 -> x19, starting transfers between devices: 15.8 us -> 25.3 us  [shift(): lax.ppermute(values, axis, [(i, (i + step) % count) for i in range(count)])]
    all_gather x2 -> x0, waiting for transfers between devices: 9.02 us -> none  [the longest x1 9.02 us: body(): text_all = lax.all_gather(text_rows, Z, axis=0)]
    pallas_call x1 -> x11, Pallas kernels: 46 us -> 37.4 us  [the longest x4 21.9 us: attend(): pl.pallas_call(functools.partial(attend_kernel, step), out_shape=jax.Shap...]
    all_to_all x1 -> x2, starting transfers between devices: 6.02 us -> 13.2 us  [the longest x1 7.39 us: body(): text_all = lax.all_to_all(text_rows, Z, 0, 0, tiled=True)]
    concatenate x4 -> x0, local copies, waits for them, and re-layouts: 6 us -> none  [the longest x1 3.36 us: body(): jnp.concatenate([rows.reshape(8, TOK, TOK), jnp.broadcast_to(squares[None...]
    dot_general x3 -> x0, matrix products: 5.75 us -> none  [the longest x2 5.15 us: project(): lax.dot_general(kv_weight, gained, (((1,), (1,)), ((), ())), preferred_el...]
    unnamed x35 -> x46, local copies, waits for them, and re-layouts: 9.69 us -> 14.2 us
    reduce_scatter x1 -> x0, waiting for transfers between devices: 3.82 us -> none  [body(): lax.psum_scatter(packed.reshape(-1, TOK), TP, scatter_dimension=0, tiled=...]
  transfers between devices with their start and end apart: 19 -> 21, of which waited for: 15 -> 11; matrix products, arithmetic and copies ran while one was open for 10% -> 2% of each run, Pallas kernels for 0% -> 21%
where the time goes in v2:
time: 144 us; the launch traced here: 143 us
  waiting for transfers between devices  41.6 us (29%)
  Pallas kernels  40.4 us (28%)
  starting transfers between devices  38.5 us (27%)
  local copies, waits for them, and re-layouts  14.2 us (10%)
  other arithmetic  5.54 us (4%)
  matrix products  3.08 us (2%)
    ppermute x19, starting transfers between devices, shift(): lax.ppermute(values, axis, [(i, (i + step) % count) for i in range(count)])  25.3 us
    ppermute x19, waiting for transfers between devices, shift(): lax.ppermute(values, axis, [(i, (i + step) % count) for i in range(count)])  24.5 us
    pallas_call x4, Pallas kernels, attend(): pl.pallas_call(functools.partial(attend_kernel, step), out_shape=jax.Shap...  21.9 us
    all_to_all x1, waiting for transfers between devices, body(): text_all = lax.all_to_all(text_rows, Z, 0, 0, tiled=True)  17.1 us
    unnamed x46, local copies, waits for them, and re-layouts  14.2 us
    all_to_all x1, starting transfers between devices, body(): text_all = lax.all_to_all(text_rows, Z, 0, 0, tiled=True)  7.39 us
    pallas_call x2, Pallas kernels, project(): pl.pallas_call(kernel, out_shape=(shape, shape), grid_spec=pltpu.Prefetch...  6.37 us
    all_to_all x1, starting transfers between devices, body(): images_all = lax.all_to_all(image_rows, Z, 0, 0, tiled=True)  5.84 us
  transfers between devices with their start and end apart: 21, of which 11 were waited for; matrix products, arithmetic and copies ran while one was open for 2% of the time, Pallas kernels for 21%

profile of v2, /device:TPU:224, one launch (start us, length us, event | category | flops | bytes accessed | tf_op | source)
XLA Modules:
  0.0 143.5 jit_solution(918243611192244073)
XLA Ops:
  2.5 3.1 %convolution_convert_fusion = bf16[128,1280]{1,0:T(8,128)(2,1)S(1)} fusion(bf16[640,1280]{1,0:T(8,128)(2,1)S(1)} %copy-done, bf16[1280,640]{1,0:T(8,128)(2,1)} %param.14, bf16[128,1280]{1,0:T(8,128)(2,1)} %param.11, f32[1280]{0:T(1024)} %param.13, f32[1280]{0:T(1024)} %param.12, f32[128]{0:T(128)S(1)} %add_rsqrt_fusion, f32[128]{0:T(128)S(1)} %broadcast_multiply_fusion), kind=kOutput, calls=%fused_computation | convolution fusion | flops 425902080 | bytes 3943424 | tf_op jit(solution)/shard_map/dot_general | solution.py:379
  7.1 2.8 %collective-permute-start.7 = (bf16[64,1280]{1,0:T(8,128)(2,1)S(1)}, bf16[64,1280]{1,0:T(8,128)(2,1)S(1)}, u32[]{:S(2)}, u32[]{:S(2)}) collective-permute-start(bf16[64,1280]{1,0:T(8,128)(2,1)S(1)} %fusion.27), channel_id=1, source_target_pairs={{0,6},{2,0},{4,2},{6,4},{1,7},{3,1},{5,3},{7,5},{8,14},{10,8},{12,... | collective-permute-start | bytes 491528 | tf_op jit(solution)/shard_map/ppermute | solution.py:33
  10.0 2.3 %collective-permute-start.5 = (bf16[64,1280]{1,0:T(8,128)(2,1)S(1)}, bf16[64,1280]{1,0:T(8,128)(2,1)S(1)}, u32[]{:S(2)}, u32[]{:S(2)}) collective-permute-start(bf16[64,1280]{1,0:T(8,128)(2,1)S(1)} %fusion.27), channel_id=1, source_target_pairs={{0,4},{2,6},{4,0},{6,2},{1,5},{3,7},{5,1},{7,3},{8,12},{10,14},{12... | collective-permute-start | bytes 491528 | tf_op jit(solution)/shard_map/ppermute | solution.py:33
  12.3 5.0 %collective-permute-done.7 = bf16[64,1280]{1,0:T(8,128)(2,1)S(1)} collective-permute-done((bf16[64,1280]{1,0:T(8,128)(2,1)S(1)}, bf16[64,1280]{1,0:T(8,128)(2,1)S(1)}, u32[]{:S(2)}, u32[]{:S(2)}) %collective-permute-start.7) | collective-permute-done | bytes 163872 | tf_op jit(solution)/shard_map/ppermute | solution.py:33
  17.3 3.4 %collective-permute-done.6 = bf16[64,1280]{1,0:T(8,128)(2,1)S(1)} collective-permute-done((bf16[64,1280]{1,0:T(8,128)(2,1)S(1)}, bf16[64,1280]{1,0:T(8,128)(2,1)S(1)}, u32[]{:S(2)}, u32[]{:S(2)}) %collective-permute-start.6) | collective-permute-done | bytes 163872 | tf_op jit(solution)/shard_map/ppermute | solution.py:33
  22.3 2.2 %copy-done.1 = bf16[2048,1024]{1,0:T(8,128)(2,1)S(1)} copy-done((bf16[2048,1024]{1,0:T(8,128)(2,1)S(1)}, bf16[2048,1024]{1,0:T(8,128)(2,1)}, u32[]{:S(2)}) %copy-start.1) | copy-done | bytes 4194328
  26.2 3.2 %shard_map.110 = (bf16[4,272,128]{2,1,0:T(8,128)(2,1)S(1)}, bf16[4,272,128]{2,1,0:T(8,128)(2,1)S(1)}) custom-call(s32[1]{0:T(128)} %bitcast.3.core, bf16[64,1280]{1,0:T(8,128)(2,1)S(1)} %fusion.11.half_ref, bf16[64,1280]{1,0:T(8,128)(2,1)S(1)} %collective-permute-done.8.other_ref, bf16[1280,1024]{1,0:T(8,128)(2,1)S(1)} %copy-done.3, f32[1,1024]{1,0:T(1,128)S(1)} %bitcast.18, ...), custom_call_target="tpu_custom_call" | custom-call | tf_op jit(solution)/shard_map/pallas_call | solution.py:116
  35.4 2.6 %collective-permute-start.12 = (bf16[272,128]{1,0:T(8,128)(2,1)}, bf16[272,128]{1,0:T(8,128)(2,1)S(1)}, u32[]{:S(2)}, u32[]{:S(2)}) collective-permute-start(bf16[272,128]{1,0:T(8,128)(2,1)} %get-tuple-element.30), channel_id=1, source_target_pairs={{0,6},{2,0},{4,2},{6,4},{1,7},{3,1},{5,3},{7,5},{8,14},{10,8},{12,... | collective-permute-start | bytes 208904 | tf_op jit(solution)/shard_map/ppermute | solution.py:33
  38.0 2.9 %collective-permute-done.10.refs_1_ = bf16[272,128]{1,0:T(8,128)(2,1)S(1)} collective-permute-done((bf16[272,128]{1,0:T(8,128)(2,1)}, bf16[272,128]{1,0:T(8,128)(2,1)S(1)}, u32[]{:S(2)}, u32[]{:S(2)}) %collective-permute-start.10) | collective-permute-done | bytes 69664 | tf_op jit(solution)/shard_map/ppermute | solution.py:33
  44.2 5.8 %all-to-all-start.1 = ((bf16[8,256,128]{2,1,0:T(8,128)(2,1)}), bf16[8,256,128]{2,1,0:T(8,128)(2,1)S(1)}, u32[]{:S(2)}, u32[]{:S(2)}) async-start(bf16[8,256,128]{2,1,0:T(8,128)(2,1)} %finish_rows.3), calls=%async_computation.1 | async-start | bytes 1048576 | tf_op jit(solution)/shard_map/all_to_all | solution.py:398
  52.2 3.2 %shard_map.109 = (bf16[4,272,256]{2,1,0:T(8,128)(2,1)S(1)}, bf16[4,272,256]{2,1,0:T(8,128)(2,1)S(1)}) custom-call(s32[1]{0:T(128)} %bitcast.3.core, bf16[256,1024]{1,0:T(8,128)(2,1)S(1)} %copy-done.7, f32[1,1024]{1,0:T(1,128)S(1)} %bitcast.19, bf16[2048,1024]{1,0:T(8,128)(2,1)S(1)} %copy-done.2), custom_call_target="tpu_custom_call" | custom-call | tf_op jit(solution)/shard_map/pallas_call | solution.py:116
  65.2 4.2 %collective-permute-done.1.refs_1_ = bf16[272,256]{1,0:T(8,128)(2,1)S(1)} collective-permute-done((bf16[272,256]{1,0:T(8,128)(2,1)}, bf16[272,256]{1,0:T(8,128)(2,1)S(1)}, u32[]{:S(2)}, u32[]{:S(2)}) %collective-permute-start.1) | collective-permute-done | bytes 139296 | tf_op jit(solution)/shard_map/ppermute | solution.py:33
  72.3 2.3 %finish_rows.2 = bf16[8,272,256]{2,1,0:T(8,128)(2,1)} custom-call(s32[2]{0:T(128)} %slots.3, f32[272,256]{1,0:T(8,128)} %get-tuple-element.21.refs_0_, bf16[272,256]{1,0:T(8,128)(2,1)} %copy-done.17, bf16[272,256]{1,0:T(8,128)(2,1)} %copy-done.18, bf16[272,256]{1,0:T(8,128)(2,1)} %copy-done.19), custom_call_target="tpu_custom_call" | custom-call | tf_op jit(solution)/shard_map/finish_rows/pallas_call | solution.py:179
  74.5 7.4 %all-to-all-start = ((bf16[8,272,256]{2,1,0:T(8,128)(2,1)}), bf16[8,272,256]{2,1,0:T(8,128)(2,1)S(1)}, u32[]{:S(2)}, u32[]{:S(2)}) async-start(bf16[8,272,256]{2,1,0:T(8,128)(2,1)} %finish_rows.2), calls=%async_computation | async-start | bytes 2228224 | tf_op jit(solution)/shard_map/all_to_all | solution.py:373
  81.9 3.2 %collective-permute-start.13 = (bf16[256,512]{1,0:T(8,128)(2,1)S(1)}, bf16[256,512]{1,0:T(8,128)(2,1)}, u32[]{:S(2)}, u32[]{:S(2)}) collective-permute-start(bf16[256,512]{1,0:T(8,128)(2,1)S(1)} %copy-done.11), channel_id=1, source_target_pairs={{0,16},{8,24},{16,0},{24,8},{1,17},{9,25},{17,1},{25,9},{2,18},{10... | collective-permute-start | bytes 786440 | tf_op jit(solution)/shard_map/ppermute | solution.py:33
  87.2 2.8 %multiply_sine_fusion = (f32[64,2048]{1,0:T(8,128)}, f32[64,2048]{1,0:T(8,128)}) fusion(f32[64]{0:T(128)S(1)} %multiply_exponential_fusion, f32[2048]{0:T(1024)S(1)} %fusion.68), kind=kLoop, calls=%fused_computation.5 | loop fusion | flops 131072 | bytes 1057024 | tf_op jit(solution)/shard_map/sin | solution.py:406
  90.1 17.1 %all-to-all-done.text_ref = bf16[8,272,256]{2,1,0:T(8,128)(2,1)S(1)} async-done(((bf16[8,272,256]{2,1,0:T(8,128)(2,1)}), bf16[8,272,256]{2,1,0:T(8,128)(2,1)S(1)}, u32[]{:S(2)}, u32[]{:S(2)}) %all-to-all-start) | async-done | bytes 1114144 | tf_op jit(solution)/shard_map/all_to_all | solution.py:373
  110.2 5.5 %attend.5 = bf16[272,512]{1,0:T(8,128)(2,1)S(1)} custom-call(s32[2]{0:T(128)S(1)} %pad_add_fusion.place, bf16[128,2048]{1,0:T(8,128)(2,1)S(1)} %get-tuple-element.31.keys, bf16[2048,256]{1,0:T(8,128)(2,1)S(1)} %get-tuple-element.32.values, bf16[256,512]{1,0:T(8,128)(2,1)} %collective-permute-done.13.query_ref), custom_call_target="tpu_custom_call" | custom-call | flops 1073741824 | bytes 2097152 | tf_op jit(solution)/shard_map/attend/pallas_call | solution.py:300
  115.8 3.3 %collective-permute-start.14 = (bf16[272,512]{1,0:T(8,128)(2,1)S(1)}, bf16[272,512]{1,0:T(8,128)(2,1)S(1)}, u32[]{:S(2)}, u32[]{:S(2)}) collective-permute-start(bf16[272,512]{1,0:T(8,128)(2,1)S(1)} %attend.5), channel_id=1, source_target_pairs={{0,16},{8,24},{16,0},{24,8},{1,17},{9,25},{17,1},{25,9},{2,18},{10... | collective-permute-start | bytes 835592 | tf_op jit(solution)/shard_map/ppermute | solution.py:33
  119.1 5.5 %attend.6 = bf16[272,512]{1,0:T(8,128)(2,1)S(1)} custom-call(s32[2]{0:T(128)S(1)} %pad_add_fusion.place, bf16[128,2048]{1,0:T(8,128)(2,1)S(1)} %get-tuple-element.31.keys, bf16[2048,256]{1,0:T(8,128)(2,1)S(1)} %get-tuple-element.32.values, bf16[256,512]{1,0:T(8,128)(2,1)} %collective-permute-done.15.query_ref), custom_call_target="tpu_custom_call" | custom-call | flops 1073741824 | bytes 2097152 | tf_op jit(solution)/shard_map/attend/pallas_call | solution.py:300
  125.4 5.5 %attend.7 = bf16[272,512]{1,0:T(8,128)(2,1)S(1)} custom-call(s32[2]{0:T(128)S(1)} %pad_add_fusion.place, bf16[128,2048]{1,0:T(8,128)(2,1)S(1)} %get-tuple-element.31.keys, bf16[2048,256]{1,0:T(8,128)(2,1)S(1)} %get-tuple-element.32.values, bf16[256,512]{1,0:T(8,128)(2,1)} %collective-permute-done.17.query_ref), custom_call_target="tpu_custom_call" | custom-call | flops 1073741824 | bytes 2097152 | tf_op jit(solution)/shard_map/attend/pallas_call | solution.py:300
  130.9 2.6 %collective-permute-start.18 = (bf16[272,512]{1,0:T(8,128)(2,1)S(1)}, bf16[272,512]{1,0:T(8,128)(2,1)}, u32[]{:S(2)}, u32[]{:S(2)}) collective-permute-start(bf16[272,512]{1,0:T(8,128)(2,1)S(1)} %attend.7), channel_id=1, source_target_pairs={{0,24},{8,0},{16,8},{24,16},{1,25},{9,1},{17,9},{25,17},{2,26},{10... | collective-permute-start | bytes 835592 | tf_op jit(solution)/shard_map/ppermute | solution.py:33
  133.6 5.3 %attend.4.refs_0_ = bf16[272,512]{1,0:T(8,128)(2,1)S(1)} custom-call(s32[2]{0:T(128)S(1)} %pad_add_fusion.place, bf16[128,2048]{1,0:T(8,128)(2,1)S(1)} %get-tuple-element.31.keys, bf16[2048,256]{1,0:T(8,128)(2,1)S(1)} %get-tuple-element.32.values, bf16[256,512]{1,0:T(8,128)(2,1)S(1)} %copy-done.11), custom_call_target="tpu_custom_call" | custom-call | flops 1073741824 | bytes 2097152 | tf_op jit(solution)/shard_map/attend/pallas_call | solution.py:300
  140.5 3.0 %combine.1 = bf16[256,512]{1,0:T(8,128)(2,1)} custom-call(bf16[272,512]{1,0:T(8,128)(2,1)} %copy-done.9, bf16[272,512]{1,0:T(8,128)(2,1)} %copy-done.15, bf16[272,512]{1,0:T(8,128)(2,1)} %copy-done.16, bf16[272,512]{1,0:T(8,128)(2,1)} %collective-permute-done.18.refs_3_), custom_call_target="tpu_custom_call" | custom-call | tf_op jit(solution)/shard_map/combine/pallas_call | solution.py:348
  (88 shorter events, 38.9 us)
Async XLA Ops:
  2.5 18.2 %copy-start.12 = (bf16[128,1280]{1,0:T(8,128)(2,1)S(1)}, bf16[128,1280]{1,0:T(8,128)(2,1)}, u32[]{:S(2)}) copy-start(bf16[128,1280]{1,0:T(8,128)(2,1)} %param.11) | copy-start | bytes 983044
  5.6 16.7 %copy-start.10 = (f32[1024]{0:T(1024)S(1)}, f32[1024]{0:T(1024)}, u32[]{:S(2)}) copy-start(f32[1024]{0:T(1024)} %param.19) | copy-start | bytes 12292
  5.6 1.5 %collective-permute-start.4 = (bf16[64,1280]{1,0:T(8,128)(2,1)S(1)}, bf16[64,1280]{1,0:T(8,128)(2,1)S(1)}, u32[]{:S(2)}, u32[]{:S(2)}) collective-permute-start(bf16[64,1280]{1,0:T(8,128)(2,1)S(1)} %dynamic-slice_bitcast_fusion), channel_id=1, source_target_pairs={{0,1},{1,0},{2,3},{3,2},{4,5},{5,4},{6,7},{7,6},{8,9},{9,8},{10,11... | collective-permute-start | bytes 491528 | tf_op jit(solution)/shard_map/ppermute | solution.py:33
  7.1 10.1 %collective-permute-start.7 = (bf16[64,1280]{1,0:T(8,128)(2,1)S(1)}, bf16[64,1280]{1,0:T(8,128)(2,1)S(1)}, u32[]{:S(2)}, u32[]{:S(2)}) collective-permute-start(bf16[64,1280]{1,0:T(8,128)(2,1)S(1)} %fusion.27), channel_id=1, source_target_pairs={{0,6},{2,0},{4,2},{6,4},{1,7},{3,1},{5,3},{7,5},{8,14},{10,8},{12,... | collective-permute-start | bytes 491528 | tf_op jit(solution)/shard_map/ppermute | solution.py:33
  10.0 10.7 %collective-permute-start.6 = (bf16[64,1280]{1,0:T(8,128)(2,1)S(1)}, bf16[64,1280]{1,0:T(8,128)(2,1)S(1)}, u32[]{:S(2)}, u32[]{:S(2)}) collective-permute-start(bf16[64,1280]{1,0:T(8,128)(2,1)S(1)} %fusion.27), channel_id=1, source_target_pairs={{0,2},{2,4},{4,6},{6,0},{1,3},{3,5},{5,7},{7,1},{8,10},{10,12},{12... | collective-permute-start | bytes 491528 | tf_op jit(solution)/shard_map/ppermute | solution.py:33
  10.0 10.7 %collective-permute-start.5 = (bf16[64,1280]{1,0:T(8,128)(2,1)S(1)}, bf16[64,1280]{1,0:T(8,128)(2,1)S(1)}, u32[]{:S(2)}, u32[]{:S(2)}) collective-permute-start(bf16[64,1280]{1,0:T(8,128)(2,1)S(1)} %fusion.27), channel_id=1, source_target_pairs={{0,4},{2,6},{4,0},{6,2},{1,5},{3,7},{5,1},{7,3},{8,12},{10,14},{12... | collective-permute-start | bytes 491528 | tf_op jit(solution)/shard_map/ppermute | solution.py:33
  20.8 1.5 %collective-permute-start.8 = (bf16[64,1280]{1,0:T(8,128)(2,1)S(1)}, bf16[64,1280]{1,0:T(8,128)(2,1)S(1)}, u32[]{:S(2)}, u32[]{:S(2)}) collective-permute-start(bf16[64,1280]{1,0:T(8,128)(2,1)S(1)} %fusion.11.half_ref), channel_id=1, source_target_pairs={{0,1},{1,0},{2,3},{3,2},{4,5},{5,4},{6,7},{7,6},{8,9},{9,8},{10,11... | collective-permute-start | bytes 491528 | tf_op jit(solution)/shard_map/ppermute | solution.py:33
  30.1 19.9 %copy-start.7 = (bf16[256,1024]{1,0:T(8,128)(2,1)S(1)}, bf16[256,1024]{1,0:T(8,128)(2,1)}, u32[]{:S(2)}) copy-start(bf16[256,1024]{1,0:T(8,128)(2,1)} %hidden_ref.1) | copy-start | bytes 1572868
  30.1 1.6 %collective-permute-start.9 = (bf16[4,272,128]{2,1,0:T(8,128)(2,1)S(1)}, bf16[4,272,128]{2,1,0:T(8,128)(2,1)S(1)}, u32[]{:S(2)}, u32[]{:S(2)}) collective-permute-start(bf16[4,272,128]{2,1,0:T(8,128)(2,1)S(1)} %get-tuple-element.26), channel_id=1, source_target_pairs={{0,1},{1,0},{2,3},{3,2},{4,5},{5,4},{6,7},{7,6},{8,9},{9,8},{10,11... | collective-permute-start | bytes 835592 | tf_op jit(solution)/shard_map/ppermute | solution.py:33
  34.2 6.7 %collective-permute-start.10 = (bf16[272,128]{1,0:T(8,128)(2,1)}, bf16[272,128]{1,0:T(8,128)(2,1)S(1)}, u32[]{:S(2)}, u32[]{:S(2)}) collective-permute-start(bf16[272,128]{1,0:T(8,128)(2,1)} %get-tuple-element.28), channel_id=1, source_target_pairs={{0,4},{2,6},{4,0},{6,2},{1,5},{3,7},{5,1},{7,3},{8,12},{10,14},{12... | collective-permute-start | bytes 208904 | tf_op jit(solution)/shard_map/ppermute | solution.py:33
  34.8 6.9 %collective-permute-start.11 = (bf16[272,128]{1,0:T(8,128)(2,1)}, bf16[272,128]{1,0:T(8,128)(2,1)S(1)}, u32[]{:S(2)}, u32[]{:S(2)}) collective-permute-start(bf16[272,128]{1,0:T(8,128)(2,1)} %get-tuple-element.29), channel_id=1, source_target_pairs={{0,2},{2,4},{4,6},{6,0},{1,3},{3,5},{5,7},{7,1},{8,10},{10,12},{12... | collective-permute-start | bytes 208904 | tf_op jit(solution)/shard_map/ppermute | solution.py:33
  35.4 6.2 %collective-permute-start.12 = (bf16[272,128]{1,0:T(8,128)(2,1)}, bf16[272,128]{1,0:T(8,128)(2,1)S(1)}, u32[]{:S(2)}, u32[]{:S(2)}) collective-permute-start(bf16[272,128]{1,0:T(8,128)(2,1)} %get-tuple-element.30), channel_id=1, source_target_pairs={{0,6},{2,0},{4,2},{6,4},{1,7},{3,1},{5,3},{7,5},{8,14},{10,8},{12,... | collective-permute-start | bytes 208904 | tf_op jit(solution)/shard_map/ppermute | solution.py:33
  44.2 30.3 %all-to-all-start.1 = ((bf16[8,256,128]{2,1,0:T(8,128)(2,1)}), bf16[8,256,128]{2,1,0:T(8,128)(2,1)S(1)}, u32[]{:S(2)}, u32[]{:S(2)}) async-start(bf16[8,256,128]{2,1,0:T(8,128)(2,1)} %finish_rows.3), calls=%async_computation.1 | async-start | bytes 1048576 | tf_op jit(solution)/shard_map/all_to_all | solution.py:398
  56.2 2.0 %collective-permute-start = (bf16[4,272,256]{2,1,0:T(8,128)(2,1)S(1)}, bf16[4,272,256]{2,1,0:T(8,128)(2,1)S(1)}, u32[]{:S(2)}, u32[]{:S(2)}) collective-permute-start(bf16[4,272,256]{2,1,0:T(8,128)(2,1)S(1)} %get-tuple-element.20), channel_id=1, source_target_pairs={{0,1},{1,0},{2,3},{3,2},{4,5},{5,4},{6,7},{7,6},{8,9},{9,8},{10,11... | collective-permute-start | bytes 1671176 | tf_op jit(solution)/shard_map/ppermute | solution.py:33
  61.1 8.3 %collective-permute-start.1 = (bf16[272,256]{1,0:T(8,128)(2,1)}, bf16[272,256]{1,0:T(8,128)(2,1)S(1)}, u32[]{:S(2)}, u32[]{:S(2)}) collective-permute-start(bf16[272,256]{1,0:T(8,128)(2,1)} %get-tuple-element.22), channel_id=1, source_target_pairs={{0,4},{2,6},{4,0},{6,2},{1,5},{3,7},{5,1},{7,3},{8,12},{10,14},{12... | collective-permute-start | bytes 417800 | tf_op jit(solution)/shard_map/ppermute | solution.py:33
  62.0 9.6 %collective-permute-start.2 = (bf16[272,256]{1,0:T(8,128)(2,1)}, bf16[272,256]{1,0:T(8,128)(2,1)S(1)}, u32[]{:S(2)}, u32[]{:S(2)}) collective-permute-start(bf16[272,256]{1,0:T(8,128)(2,1)} %get-tuple-element.23), channel_id=1, source_target_pairs={{0,2},{2,4},{4,6},{6,0},{1,3},{3,5},{5,7},{7,1},{8,10},{10,12},{12... | collective-permute-start | bytes 417800 | tf_op jit(solution)/shard_map/ppermute | solution.py:33
  64.1 7.5 %collective-permute-start.3 = (bf16[272,256]{1,0:T(8,128)(2,1)}, bf16[272,256]{1,0:T(8,128)(2,1)S(1)}, u32[]{:S(2)}, u32[]{:S(2)}) collective-permute-start(bf16[272,256]{1,0:T(8,128)(2,1)} %get-tuple-element.24), channel_id=1, source_target_pairs={{0,6},{2,0},{4,2},{6,4},{1,7},{3,1},{5,3},{7,5},{8,14},{10,8},{12,... | collective-permute-start | bytes 417800 | tf_op jit(solution)/shard_map/ppermute | solution.py:33
  74.5 32.6 %all-to-all-start = ((bf16[8,272,256]{2,1,0:T(8,128)(2,1)}), bf16[8,272,256]{2,1,0:T(8,128)(2,1)S(1)}, u32[]{:S(2)}, u32[]{:S(2)}) async-start(bf16[8,272,256]{2,1,0:T(8,128)(2,1)} %finish_rows.2), calls=%async_computation | async-start | bytes 2228224 | tf_op jit(solution)/shard_map/all_to_all | solution.py:373
  81.9 28.3 %collective-permute-start.13 = (bf16[256,512]{1,0:T(8,128)(2,1)S(1)}, bf16[256,512]{1,0:T(8,128)(2,1)}, u32[]{:S(2)}, u32[]{:S(2)}) collective-permute-start(bf16[256,512]{1,0:T(8,128)(2,1)S(1)} %copy-done.11), channel_id=1, source_target_pairs={{0,16},{8,24},{16,0},{24,8},{1,17},{9,25},{17,1},{25,9},{2,18},{10... | collective-permute-start | bytes 786440 | tf_op jit(solution)/shard_map/ppermute | solution.py:33
  85.2 34.0 %collective-permute-start.15 = (bf16[256,512]{1,0:T(8,128)(2,1)S(1)}, bf16[256,512]{1,0:T(8,128)(2,1)}, u32[]{:S(2)}, u32[]{:S(2)}) collective-permute-start(bf16[256,512]{1,0:T(8,128)(2,1)S(1)} %copy-done.11), channel_id=1, source_target_pairs={{0,24},{8,0},{16,8},{24,16},{1,25},{9,1},{17,9},{25,17},{2,26},{10... | collective-permute-start | bytes 786440 | tf_op jit(solution)/shard_map/ppermute | solution.py:33
  86.2 39.2 %collective-permute-start.17 = (bf16[256,512]{1,0:T(8,128)(2,1)S(1)}, bf16[256,512]{1,0:T(8,128)(2,1)}, u32[]{:S(2)}, u32[]{:S(2)}) collective-permute-start(bf16[256,512]{1,0:T(8,128)(2,1)S(1)} %copy-done.11), channel_id=1, source_target_pairs={{0,8},{8,16},{16,24},{24,0},{1,9},{9,17},{17,25},{25,1},{2,10},{10... | collective-permute-start | bytes 786440 | tf_op jit(solution)/shard_map/ppermute | solution.py:33
  115.8 23.9 %collective-permute-start.14 = (bf16[272,512]{1,0:T(8,128)(2,1)S(1)}, bf16[272,512]{1,0:T(8,128)(2,1)S(1)}, u32[]{:S(2)}, u32[]{:S(2)}) collective-permute-start(bf16[272,512]{1,0:T(8,128)(2,1)S(1)} %attend.5), channel_id=1, source_target_pairs={{0,16},{8,24},{16,0},{24,8},{1,17},{9,25},{17,1},{25,9},{2,18},{10... | collective-permute-start | bytes 835592 | tf_op jit(solution)/shard_map/ppermute | solution.py:33
  124.6 15.0 %collective-permute-start.16 = (bf16[272,512]{1,0:T(8,128)(2,1)S(1)}, bf16[272,512]{1,0:T(8,128)(2,1)S(1)}, u32[]{:S(2)}, u32[]{:S(2)}) collective-permute-start(bf16[272,512]{1,0:T(8,128)(2,1)S(1)} %attend.6), channel_id=1, source_target_pairs={{0,8},{8,16},{16,24},{24,0},{1,9},{9,17},{17,25},{25,1},{2,10},{10... | collective-permute-start | bytes 835592 | tf_op jit(solution)/shard_map/ppermute | solution.py:33
  130.9 9.5 %collective-permute-start.18 = (bf16[272,512]{1,0:T(8,128)(2,1)S(1)}, bf16[272,512]{1,0:T(8,128)(2,1)}, u32[]{:S(2)}, u32[]{:S(2)}) collective-permute-start(bf16[272,512]{1,0:T(8,128)(2,1)S(1)} %attend.7), channel_id=1, source_target_pairs={{0,24},{8,0},{16,8},{24,16},{1,25},{9,1},{17,9},{25,17},{2,26},{10... | collective-permute-start | bytes 835592 | tf_op jit(solution)/shard_map/ppermute | solution.py:33
  (20 other events, 31.2 us)

commit v3 on v2

--- a/solution.py
+++ b/solution.py
@@ -134,7 +134,7 @@
                 pltpu.VMEM((16, count), BF16),
             ],
         ),
-        compiler_params=vmem(24),
+        compiler_params=vmem(56),
     )(mine, *features, norm_gain[None, :], kv_weight)
 
 
@@ -154,6 +154,7 @@
             pl.BlockSpec(memory_space=pltpu.SMEM),
             *[pl.BlockSpec(memory_space=pltpu.VMEM)] * 2,
         ],
+        compiler_params=vmem(6),
         name="add_pair",
     )(jnp.reshape(x_at, (1,)).astype(jnp.int32), keep, got)
 
@@ -183,15 +184,14 @@
             pl.BlockSpec(memory_space=pltpu.SMEM),
             *[pl.BlockSpec(memory_space=pltpu.VMEM)] * 4,
         ],
+        compiler_params=vmem(6),
         name="finish_rows",
     )(slots, *pieces)
 
 
-def scatter_rows(give, keep, slots, x_at, row_count):
-    got = shift(give, "core", 1)
-    own, two, one, three = add_pair(keep, got, x_at)
-    pieces = [own, shift(two, "x", 2), shift(one, "x", 1), shift(three, "x", 3)]
-    return finish_rows(slots, pieces, row_count)
+def exchange(pieces):
+    own, two, one, three = pieces
+    return [own, shift(two, "x", 2), shift(one, "x", 1), shift(three, "x", 3)]
 
 
 def merge_kernel(text_ref, image_ref, cos_ref, sin_ref, keys, values):
@@ -207,7 +207,7 @@
                 rows = jnp.where(
                     source == float(r), image_ref[2 * r + block % 2].astype(F32), rows
                 )
-            cosine, sine = cos_ref[:, here], sin_ref[:, here]
+            cosine, sine = cos_ref[:, here] * (SCALE * LOG2E), sin_ref[:, here] * (SCALE * LOG2E)
             first, second = rows[:HALF], rows[HALF:HEAD]
             keys[:HALF, here] = (first * cosine - second * sine).astype(BF16)
             keys[HALF:, here] = (second * cosine + first * sine).astype(BF16)
@@ -221,7 +221,7 @@
             jax.ShapeDtypeStruct((HEAD, KEYS), BF16),
             jax.ShapeDtypeStruct((KEYS, 2 * HEAD), BF16),
         ),
-        compiler_params=vmem(24),
+        compiler_params=vmem(10),
         name="merge",
     )(text, images, cosine, sine)
 
@@ -267,7 +267,7 @@
     def last():
         score(plain, True)
 
-    offset = jnp.max(top[...], axis=1, keepdims=True) * (SCALE * LOG2E)
+    offset = jnp.max(top[...], axis=1, keepdims=True)
     top[...] = jnp.broadcast_to(offset, top.shape)
 
     @pl.loop(0, chunks)
@@ -276,7 +276,7 @@
         values_now = values[at, :]
         for h in range(GROUP):
             here = slice(h * TOK, (h + 1) * TOK)
-            weights = jnp.exp2(scores[here, at] * (SCALE * LOG2E) - top[here, :1]).astype(BF16)
+            weights = jnp.exp2(scores[here, at] - top[here, :1]).astype(BF16)
             mixed[here, :] += jnp.dot(weights, values_now, preferred_element_type=F32)
 
     lane = lax.broadcasted_iota(jnp.int32, (TOK, HEAD), 1)
@@ -310,7 +310,7 @@
             pltpu.VMEM((ROWS_Q, HEAD), F32),
             pltpu.VMEM((ROWS_Q, 2 * HEAD), F32),
         ],
-        compiler_params=vmem(40),
+        compiler_params=vmem(24),
         cost_estimate=pl.CostEstimate(
             flops=4 * ROWS_Q * KEYS * HEAD, bytes_accessed=2 << 20, transcendentals=ROWS_Q * KEYS
         ),
@@ -326,28 +326,34 @@
 
 
 def combine_kernel(*refs):
-    out_ref = refs[-1]
+    *parts, out_ref = refs
     levels = []
-    for ref in refs[:-1]:
+    for ref in parts:
         rows = ref[TOK:, :TOK].astype(F32)
-        levels.append(jnp.concatenate([rows, jnp.zeros((HEAD - rows.shape[0], TOK), F32)], 0).T)
+        levels.append(
+            [rows[3 * h : 3 * h + 1] + rows[3 * h + 1 : 3 * h + 2] + rows[3 * h + 2 : 3 * h + 3] for h in range(GROUP)]
+        )
+    weights = []
+    for h in range(GROUP):
+        most = functools.reduce(jnp.maximum, [level[h] for level in levels])
+        raised = [jnp.exp2(level[h] - most) for level in levels]
+        total = sum(raised)
+        weights += [r / total for r in raised]
+    rows = jnp.concatenate([*weights, jnp.zeros((HEAD - len(weights), TOK), F32)], 0).T
     for h in range(GROUP):
         lanes = slice(h * HEAD, (h + 1) * HEAD)
-        level = [
-            l[:, 3 * h : 3 * h + 1] + l[:, 3 * h + 1 : 3 * h + 2] + l[:, 3 * h + 2 : 3 * h + 3]
-            for l in levels
-        ]
-        most = functools.reduce(jnp.maximum, level)
-        weights = [jnp.exp2(l - most) for l in level]
-        total = sum(weights)
-        mixed = sum(w * ref[:TOK, lanes].astype(F32) for w, ref in zip(weights, refs[:-1]))
-        out_ref[:, lanes] = (mixed / total).astype(BF16)
+        mixed = sum(
+            rows[:, 4 * h + i : 4 * h + i + 1] * ref[:TOK, lanes].astype(F32)
+            for i, ref in enumerate(parts)
+        )
+        out_ref[:, lanes] = mixed.astype(BF16)
 
 
 def combine(parts):
     return pl.pallas_call(
         combine_kernel,
         out_shape=jax.ShapeDtypeStruct((TOK, GROUP * HEAD), BF16),
+        compiler_params=vmem(6),
         name="combine",
     )(*parts)
 
@@ -369,8 +375,8 @@
     x_at, core = lax.axis_index("x"), lax.axis_index("core")
 
     give, keep = project(text_project_kernel, [hidden_text], norm_gain, kv_weight, core, TOK, [])
-    text_rows = scatter_rows(give, keep, slot_source, x_at, ROWS)
-    text_all = lax.all_to_all(text_rows, Z, 0, 0, tiled=True)
+    patches, give, keep = lax.optimization_barrier((patches, give, keep))
+    text_pieces = add_pair(keep, shift(give, "core", 1), x_at)
 
     normed_patches = layer_norm(patches, patch_gain, patch_shift)
     enc_hidden = jax.nn.gelu(
@@ -379,10 +385,15 @@
     partial_out = jnp.dot(enc_hidden, encoder_down, preferred_element_type=F32).astype(BF16)
     halves = partial_out.reshape(2, HALF, -1)
     half = pick(halves, core).astype(F32) + shift(pick(halves, 1 - core), "core", 1).astype(F32)
+    half, text_pieces = lax.optimization_barrier((half, text_pieces))
+    text_got = exchange(text_pieces)
     sent = half.astype(BF16)
     for step in (2, 1, 3):
         half = half + shift(sent, "x", step).astype(F32)
     half = (half + pick(patches.reshape(2, HALF, -1), core).astype(F32)).astype(BF16)
+    text_rows = finish_rows(slot_source, text_got, ROWS)
+    half, text_rows = lax.optimization_barrier((half, text_rows))
+    text_all = lax.all_to_all(text_rows, Z, 0, 0, tiled=True)
     other = shift(half, "core", 1)
 
     give, keep = project(
@@ -394,7 +405,10 @@
         IMG,
         [pltpu.VMEM(patches.shape, BF16)],
     )
-    image_rows = scatter_rows(give, keep, slot_source, x_at, TOK)
+    asked = {step: shift(queries, "y", 4 - step) for step in (2, 1, 3)}
+    image_got = exchange(add_pair(keep, shift(give, "core", 1), x_at))
+    image_rows = finish_rows(slot_source, image_got, TOK)
+    image_rows, text_all, asked = lax.optimization_barrier((image_rows, text_all, asked))
     images_all = lax.all_to_all(image_rows, Z, 0, 0, tiled=True)
 
     frequencies = jnp.exp(
@@ -407,8 +421,7 @@
     place = jnp.stack([z_at, y_at]).astype(jnp.int32)
     received = []
     for step in (2, 1, 3):
-        asked = shift(queries, "y", 4 - step)
-        received.append(shift(attend(step, place, keys, values, asked), "y", step))
+        received.append(shift(attend(step, place, keys, values, asked[step]), "y", step))
     return combine([attend(0, place, keys, values, queries), *received])
 
 

time: 144 us -> 126 us (0.88)
  the two profiles are of different devices: /device:TPU:224 before, /device:TPU:198 now
where the time goes in v3:
time: 126 us; the launch traced here: 125 us
  Pallas kernels  41.6 us (33%)
  starting transfers between devices  34.7 us (28%)
  waiting for transfers between devices  33.5 us (27%)
  local copies, waits for them, and re-layouts  7.58 us (6%)
  other arithmetic  4.36 us (3%)
  matrix products  2.99 us (2%)
    ppermute x19, waiting for transfers between devices, shift(): lax.ppermute(values, axis, [(i, (i + step) % count) for i in range(count)])  24.7 us
    ppermute x19, starting transfers between devices, shift(): lax.ppermute(values, axis, [(i, (i + step) % count) for i in range(count)])  21.2 us
    pallas_call x4, Pallas kernels, attend(): pl.pallas_call(functools.partial(attend_kernel, step), out_shape=jax.Shap...  20.5 us
    pallas_call x2, Pallas kernels, project(): pl.pallas_call(kernel, out_shape=(shape, shape), grid_spec=pltpu.Prefetch...  16.4 us
    all_to_all x1, waiting for transfers between devices, body(): images_all = lax.all_to_all(image_rows, Z, 0, 0, tiled=True)  8.8 us
    all_to_all x1, starting transfers between devices, body(): images_all = lax.all_to_all(image_rows, Z, 0, 0, tiled=True)  7.2 us
    unnamed x38, local copies, waits for them, and re-layouts  6.9 us
    all_to_all x1, starting transfers between devices, body(): text_all = lax.all_to_all(text_rows, Z, 0, 0, tiled=True)  6.3 us
  transfers between devices with their start and end apart: 21, of which 10 were waited for; matrix products, arithmetic and copies ran while one was open for 3% of the time, Pallas kernels for 13%

profile of v3, /device:TPU:198, one launch (start us, length us, event | category | flops | bytes accessed | tf_op | source)
XLA Modules:
  0.0 125.0 jit_solution(1527261754159975806)
XLA Ops:
  0.0 7.8 %shard_map.109 = (bf16[4,272,256]{2,1,0:T(8,128)(2,1)}, bf16[4,272,256]{2,1,0:T(8,128)(2,1)}) custom-call(s32[1]{0:T(128)} %bitcast.3.core, bf16[256,1024]{1,0:T(8,128)(2,1)} %hidden_ref.1, f32[1,1024]{1,0:T(1,128)} %bitcast.20, bf16[2048,1024]{1,0:T(8,128)(2,1)} %weight_ref.3), custom_call_target="tpu_custom_call" | custom-call | tf_op jit(solution)/shard_map/pallas_call | solution.py:116
  8.2 3.0 %convolution_convert_fusion = bf16[128,1280]{1,0:T(8,128)(2,1)S(1)} fusion(bf16[640,1280]{1,0:T(8,128)(2,1)S(1)} %copy-done, bf16[1280,640]{1,0:T(8,128)(2,1)} %param.14, bf16[128,1280]{1,0:T(8,128)(2,1)S(1)} %copy-done.14, f32[1280]{0:T(1024)S(1)} %copy-done.17, f32[1280]{0:T(1024)S(1)} %copy-done.18, f32[128]{0:T(128)S(1)} %add_rsqrt_fusion, ...), kind=kOutput, calls=%fused_computation | convolution fusion | flops 425902080 | bytes 3943424 | tf_op jit(solution)/shard_map/dot_general | solution.py:385
  15.0 1.5 %collective-permute-start.5 = (bf16[272,256]{1,0:T(8,128)(2,1)S(1)}, bf16[272,256]{1,0:T(8,128)(2,1)S(1)}, u32[]{:S(2)}, u32[]{:S(2)}) collective-permute-start(bf16[272,256]{1,0:T(8,128)(2,1)S(1)} %get-tuple-element.45), channel_id=1, source_target_pairs={{0,4},{2,6},{4,0},{6,2},{1,5},{3,7},{5,1},{7,3},{8,12},{10,14},{12... | collective-permute-start | bytes 417800 | tf_op jit(solution)/shard_map/ppermute | solution.py:33
  16.6 3.2 %collective-permute-start.3 = (bf16[64,1280]{1,0:T(8,128)(2,1)S(1)}, bf16[64,1280]{1,0:T(8,128)(2,1)S(1)}, u32[]{:S(2)}, u32[]{:S(2)}) collective-permute-start(bf16[64,1280]{1,0:T(8,128)(2,1)S(1)} %convert_element_type.56), channel_id=1, source_target_pairs={{0,2},{2,4},{4,6},{6,0},{1,3},{3,5},{5,7},{7,1},{8,10},{10,12},{12... | collective-permute-start | bytes 491528 | tf_op jit(solution)/shard_map/ppermute | solution.py:33
  21.3 1.7 %collective-permute-done.5.refs_1_ = bf16[272,256]{1,0:T(8,128)(2,1)S(1)} collective-permute-done((bf16[272,256]{1,0:T(8,128)(2,1)S(1)}, bf16[272,256]{1,0:T(8,128)(2,1)S(1)}, u32[]{:S(2)}, u32[]{:S(2)}) %collective-permute-start.5) | collective-permute-done | bytes 139296 | tf_op jit(solution)/shard_map/ppermute | solution.py:33
  23.9 6.2 %collective-permute-done.6.refs_2_ = bf16[272,256]{1,0:T(8,128)(2,1)S(1)} collective-permute-done((bf16[272,256]{1,0:T(8,128)(2,1)S(1)}, bf16[272,256]{1,0:T(8,128)(2,1)S(1)}, u32[]{:S(2)}, u32[]{:S(2)}) %collective-permute-start.6) | collective-permute-done | bytes 139296 | tf_op jit(solution)/shard_map/ppermute | solution.py:33
  30.1 2.2 %collective-permute-done.7.refs_3_ = bf16[272,256]{1,0:T(8,128)(2,1)S(1)} collective-permute-done((bf16[272,256]{1,0:T(8,128)(2,1)S(1)}, bf16[272,256]{1,0:T(8,128)(2,1)S(1)}, u32[]{:S(2)}, u32[]{:S(2)}) %collective-permute-start.7) | collective-permute-done | bytes 139296 | tf_op jit(solution)/shard_map/ppermute | solution.py:33
  34.1 6.3 %all-to-all-start = ((bf16[8,272,256]{2,1,0:T(8,128)(2,1)}), bf16[8,272,256]{2,1,0:T(8,128)(2,1)S(1)}, u32[]{:S(2)}, u32[]{:S(2)}) async-start(bf16[8,272,256]{2,1,0:T(8,128)(2,1)} %copy-done.1), calls=%async_computation | async-start | bytes 2228224 | tf_op jit(solution)/shard_map/all_to_all | solution.py:396
  42.4 8.6 %shard_map.110 = (bf16[4,272,128]{2,1,0:T(8,128)(2,1)}, bf16[4,272,128]{2,1,0:T(8,128)(2,1)}) custom-call(s32[1]{0:T(128)} %bitcast.3.core, bf16[64,1280]{1,0:T(8,128)(2,1)} %copy-done.15, bf16[64,1280]{1,0:T(8,128)(2,1)} %copy-done.16, bf16[1280,1024]{1,0:T(8,128)(2,1)} %proj_ref.1, f32[1,1024]{1,0:T(1,128)} %bitcast.21, bf16[2048,1024]{1,0:T(8,128)(2,1)} %weight_ref.3), custom_call_target="tpu_custom_call" | custom-call | tf_op jit(solution)/shard_map/pallas_call | solution.py:116
  51.2 3.2 %collective-permute-start.14 = (bf16[256,512]{1,0:T(8,128)(2,1)S(1)}, bf16[256,512]{1,0:T(8,128)(2,1)S(1)}, u32[]{:S(2)}, u32[]{:S(2)}) collective-permute-start(bf16[256,512]{1,0:T(8,128)(2,1)S(1)} %copy-done.7), channel_id=1, source_target_pairs={{0,16},{8,24},{16,0},{24,8},{1,17},{9,25},{17,1},{25,9},{2,18},{10... | collective-permute-start | bytes 786440 | tf_op jit(solution)/shard_map/ppermute | solution.py:33
  57.4 1.8 %collective-permute-start.10 = (bf16[272,128]{1,0:T(8,128)(2,1)S(1)}, bf16[272,128]{1,0:T(8,128)(2,1)S(1)}, u32[]{:S(2)}, u32[]{:S(2)}) collective-permute-start(bf16[272,128]{1,0:T(8,128)(2,1)S(1)} %get-tuple-element.52), channel_id=1, source_target_pairs={{0,4},{2,6},{4,0},{6,2},{1,5},{3,7},{5,1},{7,3},{8,12},{10,14},{12... | collective-permute-start | bytes 208904 | tf_op jit(solution)/shard_map/ppermute | solution.py:33
  59.2 2.0 %collective-permute-start.11 = (bf16[272,128]{1,0:T(8,128)(2,1)S(1)}, bf16[272,128]{1,0:T(8,128)(2,1)S(1)}, u32[]{:S(2)}, u32[]{:S(2)}) collective-permute-start(bf16[272,128]{1,0:T(8,128)(2,1)S(1)} %get-tuple-element.53), channel_id=1, source_target_pairs={{0,2},{2,4},{4,6},{6,0},{1,3},{3,5},{5,7},{7,1},{8,10},{10,12},{12... | collective-permute-start | bytes 208904 | tf_op jit(solution)/shard_map/ppermute | solution.py:33
  61.2 2.3 %collective-permute-done.10.refs_1_ = bf16[272,128]{1,0:T(8,128)(2,1)S(1)} collective-permute-done((bf16[272,128]{1,0:T(8,128)(2,1)S(1)}, bf16[272,128]{1,0:T(8,128)(2,1)S(1)}, u32[]{:S(2)}, u32[]{:S(2)}) %collective-permute-start.10) | collective-permute-done | bytes 69664 | tf_op jit(solution)/shard_map/ppermute | solution.py:33
  64.5 4.5 %collective-permute-done.12.refs_3_ = bf16[272,128]{1,0:T(8,128)(2,1)S(1)} collective-permute-done((bf16[272,128]{1,0:T(8,128)(2,1)S(1)}, bf16[272,128]{1,0:T(8,128)(2,1)S(1)}, u32[]{:S(2)}, u32[]{:S(2)}) %collective-permute-start.12) | collective-permute-done | bytes 69664 | tf_op jit(solution)/shard_map/ppermute | solution.py:33
  72.6 7.2 %all-to-all-start.1 = ((bf16[8,256,128]{2,1,0:T(8,128)(2,1)}), bf16[8,256,128]{2,1,0:T(8,128)(2,1)S(1)}, u32[]{:S(2)}, u32[]{:S(2)}) async-start(bf16[8,256,128]{2,1,0:T(8,128)(2,1)} %finish_rows.3), calls=%async_computation.1 | async-start | bytes 1048576 | tf_op jit(solution)/shard_map/all_to_all | solution.py:412
  79.9 2.8 %multiply_sine_fusion = (f32[64,2048]{1,0:T(8,128)}, f32[64,2048]{1,0:T(8,128)}) fusion(f32[64]{0:T(128)S(1)} %multiply_exponential_fusion, f32[2048]{0:T(1024)S(1)} %fusion.67), kind=kLoop, calls=%fused_computation.5 | loop fusion | flops 131072 | bytes 1057024 | tf_op jit(solution)/shard_map/sin | solution.py:420
  82.7 8.8 %all-to-all-done.1.image_ref = bf16[8,256,128]{2,1,0:T(8,128)(2,1)S(1)} async-done(((bf16[8,256,128]{2,1,0:T(8,128)(2,1)}), bf16[8,256,128]{2,1,0:T(8,128)(2,1)S(1)}, u32[]{:S(2)}, u32[]{:S(2)}) %all-to-all-start.1) | async-done | bytes 524320 | tf_op jit(solution)/shard_map/all_to_all | solution.py:412
  94.7 5.1 %attend.7 = bf16[272,512]{1,0:T(8,128)(2,1)S(1)} custom-call(s32[2]{0:T(128)S(1)} %pad_add_fusion.place, bf16[128,2048]{1,0:T(8,128)(2,1)S(1)} %get-tuple-element.58.keys, bf16[2048,256]{1,0:T(8,128)(2,1)S(1)} %get-tuple-element.59.values, bf16[256,512]{1,0:T(8,128)(2,1)S(1)} %copy-done.13), custom_call_target="tpu_custom_call" | custom-call | flops 1073741824 | bytes 2097152 | tf_op jit(solution)/shard_map/attend/pallas_call | solution.py:300
  99.8 5.1 %attend.6 = bf16[272,512]{1,0:T(8,128)(2,1)S(1)} custom-call(s32[2]{0:T(128)S(1)} %pad_add_fusion.place, bf16[128,2048]{1,0:T(8,128)(2,1)S(1)} %get-tuple-element.58.keys, bf16[2048,256]{1,0:T(8,128)(2,1)S(1)} %get-tuple-element.59.values, bf16[256,512]{1,0:T(8,128)(2,1)S(1)} %copy-done.11), custom_call_target="tpu_custom_call" | custom-call | flops 1073741824 | bytes 2097152 | tf_op jit(solution)/shard_map/attend/pallas_call | solution.py:300
  105.0 5.1 %attend.5 = bf16[272,512]{1,0:T(8,128)(2,1)S(1)} custom-call(s32[2]{0:T(128)S(1)} %pad_add_fusion.place, bf16[128,2048]{1,0:T(8,128)(2,1)S(1)} %get-tuple-element.58.keys, bf16[2048,256]{1,0:T(8,128)(2,1)S(1)} %get-tuple-element.59.values, bf16[256,512]{1,0:T(8,128)(2,1)S(1)} %copy-done.9), custom_call_target="tpu_custom_call" | custom-call | flops 1073741824 | bytes 2097152 | tf_op jit(solution)/shard_map/attend/pallas_call | solution.py:300
  110.3 3.2 %collective-permute-start.18 = (bf16[272,512]{1,0:T(8,128)(2,1)S(1)}, bf16[272,512]{1,0:T(8,128)(2,1)S(1)}, u32[]{:S(2)}, u32[]{:S(2)}) collective-permute-start(bf16[272,512]{1,0:T(8,128)(2,1)S(1)} %attend.7), channel_id=1, source_target_pairs={{0,24},{8,0},{16,8},{24,16},{1,25},{9,1},{17,9},{25,17},{2,26},{10... | collective-permute-start | bytes 835592 | tf_op jit(solution)/shard_map/ppermute | solution.py:33
  113.5 5.1 %attend.4.refs_0_ = bf16[272,512]{1,0:T(8,128)(2,1)S(1)} custom-call(s32[2]{0:T(128)S(1)} %pad_add_fusion.place, bf16[128,2048]{1,0:T(8,128)(2,1)S(1)} %get-tuple-element.58.keys, bf16[2048,256]{1,0:T(8,128)(2,1)S(1)} %get-tuple-element.59.values, bf16[256,512]{1,0:T(8,128)(2,1)S(1)} %copy-done.7), custom_call_target="tpu_custom_call" | custom-call | flops 1073741824 | bytes 2097152 | tf_op jit(solution)/shard_map/attend/pallas_call | solution.py:300
  118.6 2.2 %collective-permute-done.16.refs_1_ = bf16[272,512]{1,0:T(8,128)(2,1)S(1)} collective-permute-done((bf16[272,512]{1,0:T(8,128)(2,1)S(1)}, bf16[272,512]{1,0:T(8,128)(2,1)S(1)}, u32[]{:S(2)}, u32[]{:S(2)}) %collective-permute-start.16) | collective-permute-done | bytes 278560 | tf_op jit(solution)/shard_map/ppermute | solution.py:33
  120.8 2.7 %collective-permute-done.17.refs_2_ = bf16[272,512]{1,0:T(8,128)(2,1)S(1)} collective-permute-done((bf16[272,512]{1,0:T(8,128)(2,1)S(1)}, bf16[272,512]{1,0:T(8,128)(2,1)S(1)}, u32[]{:S(2)}, u32[]{:S(2)}) %collective-permute-start.17) | collective-permute-done | bytes 278560 | tf_op jit(solution)/shard_map/ppermute | solution.py:33
  (81 shorter events, 23.1 us)
Async XLA Ops:
  0.0 8.2 %copy-start.18 = (f32[1280]{0:T(1024)S(1)}, f32[1280]{0:T(1024)}, u32[]{:S(2)}) copy-start(f32[1280]{0:T(1024)} %param.12) | copy-start | bytes 15364
  11.2 21.1 %copy-start.6 = (s32[2]{0:T(128)S(1)}, s32[2]{0:T(128)}, u32[]{:S(2)}) copy-start(s32[2]{0:T(128)} %slots.3) | copy-start | bytes 28
  11.9 1.9 %collective-permute-start = (bf16[64,1280]{1,0:T(8,128)(2,1)}, bf16[64,1280]{1,0:T(8,128)(2,1)}, u32[]{:S(2)}, u32[]{:S(2)}) collective-permute-start(bf16[64,1280]{1,0:T(8,128)(2,1)} %dynamic-slice_bitcast_fusion), channel_id=1, source_target_pairs={{0,1},{1,0},{2,3},{3,2},{4,5},{5,4},{6,7},{7,6},{8,9},{9,8},{10,11... | collective-permute-start | bytes 491528 | tf_op jit(solution)/shard_map/ppermute | solution.py:33
  11.9 2.9 %collective-permute-start.1 = (bf16[4,272,256]{2,1,0:T(8,128)(2,1)}, bf16[4,272,256]{2,1,0:T(8,128)(2,1)S(1)}, u32[]{:S(2)}, u32[]{:S(2)}) collective-permute-start(bf16[4,272,256]{2,1,0:T(8,128)(2,1)} %get-tuple-element.38), channel_id=1, source_target_pairs={{0,1},{1,0},{2,3},{3,2},{4,5},{5,4},{6,7},{7,6},{8,9},{9,8},{10,11... | collective-permute-start | bytes 1671176 | tf_op jit(solution)/shard_map/ppermute | solution.py:33
  15.0 8.1 %collective-permute-start.5 = (bf16[272,256]{1,0:T(8,128)(2,1)S(1)}, bf16[272,256]{1,0:T(8,128)(2,1)S(1)}, u32[]{:S(2)}, u32[]{:S(2)}) collective-permute-start(bf16[272,256]{1,0:T(8,128)(2,1)S(1)} %get-tuple-element.45), channel_id=1, source_target_pairs={{0,4},{2,6},{4,0},{6,2},{1,5},{3,7},{5,1},{7,3},{8,12},{10,14},{12... | collective-permute-start | bytes 417800 | tf_op jit(solution)/shard_map/ppermute | solution.py:33
  16.5 17.5 %collective-permute-start.4 = (bf16[64,1280]{1,0:T(8,128)(2,1)S(1)}, bf16[64,1280]{1,0:T(8,128)(2,1)S(1)}, u32[]{:S(2)}, u32[]{:S(2)}) collective-permute-start(bf16[64,1280]{1,0:T(8,128)(2,1)S(1)} %convert_element_type.56), channel_id=1, source_target_pairs={{0,6},{2,0},{4,2},{6,4},{1,7},{3,1},{5,3},{7,5},{8,14},{10,8},{12,... | collective-permute-start | bytes 491528 | tf_op jit(solution)/shard_map/ppermute | solution.py:33
  16.6 17.4 %collective-permute-start.3 = (bf16[64,1280]{1,0:T(8,128)(2,1)S(1)}, bf16[64,1280]{1,0:T(8,128)(2,1)S(1)}, u32[]{:S(2)}, u32[]{:S(2)}) collective-permute-start(bf16[64,1280]{1,0:T(8,128)(2,1)S(1)} %convert_element_type.56), channel_id=1, source_target_pairs={{0,2},{2,4},{4,6},{6,0},{1,3},{3,5},{5,7},{7,1},{8,10},{10,12},{12... | collective-permute-start | bytes 491528 | tf_op jit(solution)/shard_map/ppermute | solution.py:33
  19.8 14.2 %collective-permute-start.2 = (bf16[64,1280]{1,0:T(8,128)(2,1)S(1)}, bf16[64,1280]{1,0:T(8,128)(2,1)S(1)}, u32[]{:S(2)}, u32[]{:S(2)}) collective-permute-start(bf16[64,1280]{1,0:T(8,128)(2,1)S(1)} %convert_element_type.56), channel_id=1, source_target_pairs={{0,4},{2,6},{4,0},{6,2},{1,5},{3,7},{5,1},{7,3},{8,12},{10,14},{12... | collective-permute-start | bytes 491528 | tf_op jit(solution)/shard_map/ppermute | solution.py:33
  20.7 9.4 %collective-permute-start.6 = (bf16[272,256]{1,0:T(8,128)(2,1)S(1)}, bf16[272,256]{1,0:T(8,128)(2,1)S(1)}, u32[]{:S(2)}, u32[]{:S(2)}) collective-permute-start(bf16[272,256]{1,0:T(8,128)(2,1)S(1)} %get-tuple-element.46), channel_id=1, source_target_pairs={{0,2},{2,4},{4,6},{6,0},{1,3},{3,5},{5,7},{7,1},{8,10},{10,12},{12... | collective-permute-start | bytes 417800 | tf_op jit(solution)/shard_map/ppermute | solution.py:33
  23.1 9.2 %collective-permute-start.7 = (bf16[272,256]{1,0:T(8,128)(2,1)S(1)}, bf16[272,256]{1,0:T(8,128)(2,1)S(1)}, u32[]{:S(2)}, u32[]{:S(2)}) collective-permute-start(bf16[272,256]{1,0:T(8,128)(2,1)S(1)} %get-tuple-element.47), channel_id=1, source_target_pairs={{0,6},{2,0},{4,2},{6,4},{1,7},{3,1},{5,3},{7,5},{8,14},{10,8},{12,... | collective-permute-start | bytes 417800 | tf_op jit(solution)/shard_map/ppermute | solution.py:33
  34.1 38.5 %all-to-all-start = ((bf16[8,272,256]{2,1,0:T(8,128)(2,1)}), bf16[8,272,256]{2,1,0:T(8,128)(2,1)S(1)}, u32[]{:S(2)}, u32[]{:S(2)}) async-start(bf16[8,272,256]{2,1,0:T(8,128)(2,1)} %copy-done.1), calls=%async_computation | async-start | bytes 2228224 | tf_op jit(solution)/shard_map/all_to_all | solution.py:396
  40.4 10.8 %copy-start.7 = (bf16[256,512]{1,0:T(8,128)(2,1)S(1)}, bf16[256,512]{1,0:T(8,128)(2,1)}, u32[]{:S(2)}) copy-start(bf16[256,512]{1,0:T(8,128)(2,1)} %query_ref.1) | copy-start | bytes 786436
  40.4 1.4 %collective-permute-start.8 = (bf16[64,1280]{1,0:T(8,128)(2,1)S(1)}, bf16[64,1280]{1,0:T(8,128)(2,1)S(1)}, u32[]{:S(2)}, u32[]{:S(2)}) collective-permute-start(bf16[64,1280]{1,0:T(8,128)(2,1)S(1)} %fusion.11.half_ref), channel_id=1, source_target_pairs={{0,1},{1,0},{2,3},{3,2},{4,5},{5,4},{6,7},{7,6},{8,9},{9,8},{10,11... | collective-permute-start | bytes 491528 | tf_op jit(solution)/shard_map/ppermute | solution.py:33
  51.0 5.4 %collective-permute-start.9 = (bf16[4,272,128]{2,1,0:T(8,128)(2,1)}, bf16[4,272,128]{2,1,0:T(8,128)(2,1)S(1)}, u32[]{:S(2)}, u32[]{:S(2)}) collective-permute-start(bf16[4,272,128]{2,1,0:T(8,128)(2,1)} %get-tuple-element.50), channel_id=1, source_target_pairs={{0,1},{1,0},{2,3},{3,2},{4,5},{5,4},{6,7},{7,6},{8,9},{9,8},{10,11... | collective-permute-start | bytes 835592 | tf_op jit(solution)/shard_map/ppermute | solution.py:33
  51.2 19.3 %collective-permute-start.14 = (bf16[256,512]{1,0:T(8,128)(2,1)S(1)}, bf16[256,512]{1,0:T(8,128)(2,1)S(1)}, u32[]{:S(2)}, u32[]{:S(2)}) collective-permute-start(bf16[256,512]{1,0:T(8,128)(2,1)S(1)} %copy-done.7), channel_id=1, source_target_pairs={{0,16},{8,24},{16,0},{24,8},{1,17},{9,25},{17,1},{25,9},{2,18},{10... | collective-permute-start | bytes 786440 | tf_op jit(solution)/shard_map/ppermute | solution.py:33
  54.4 16.8 %collective-permute-start.13 = (bf16[256,512]{1,0:T(8,128)(2,1)S(1)}, bf16[256,512]{1,0:T(8,128)(2,1)S(1)}, u32[]{:S(2)}, u32[]{:S(2)}) collective-permute-start(bf16[256,512]{1,0:T(8,128)(2,1)S(1)} %copy-done.7), channel_id=1, source_target_pairs={{0,24},{8,0},{16,8},{24,16},{1,25},{9,1},{17,9},{25,17},{2,26},{10... | collective-permute-start | bytes 786440 | tf_op jit(solution)/shard_map/ppermute | solution.py:33
  55.4 16.4 %collective-permute-start.15 = (bf16[256,512]{1,0:T(8,128)(2,1)S(1)}, bf16[256,512]{1,0:T(8,128)(2,1)S(1)}, u32[]{:S(2)}, u32[]{:S(2)}) collective-permute-start(bf16[256,512]{1,0:T(8,128)(2,1)S(1)} %copy-done.7), channel_id=1, source_target_pairs={{0,8},{8,16},{16,24},{24,0},{1,9},{9,17},{17,25},{25,1},{2,10},{10... | collective-permute-start | bytes 786440 | tf_op jit(solution)/shard_map/ppermute | solution.py:33
  57.4 6.1 %collective-permute-start.10 = (bf16[272,128]{1,0:T(8,128)(2,1)S(1)}, bf16[272,128]{1,0:T(8,128)(2,1)S(1)}, u32[]{:S(2)}, u32[]{:S(2)}) collective-permute-start(bf16[272,128]{1,0:T(8,128)(2,1)S(1)} %get-tuple-element.52), channel_id=1, source_target_pairs={{0,4},{2,6},{4,0},{6,2},{1,5},{3,7},{5,1},{7,3},{8,12},{10,14},{12... | collective-permute-start | bytes 208904 | tf_op jit(solution)/shard_map/ppermute | solution.py:33
  59.2 5.3 %collective-permute-start.11 = (bf16[272,128]{1,0:T(8,128)(2,1)S(1)}, bf16[272,128]{1,0:T(8,128)(2,1)S(1)}, u32[]{:S(2)}, u32[]{:S(2)}) collective-permute-start(bf16[272,128]{1,0:T(8,128)(2,1)S(1)} %get-tuple-element.53), channel_id=1, source_target_pairs={{0,2},{2,4},{4,6},{6,0},{1,3},{3,5},{5,7},{7,1},{8,10},{10,12},{12... | collective-permute-start | bytes 208904 | tf_op jit(solution)/shard_map/ppermute | solution.py:33
  63.5 5.5 %collective-permute-start.12 = (bf16[272,128]{1,0:T(8,128)(2,1)S(1)}, bf16[272,128]{1,0:T(8,128)(2,1)S(1)}, u32[]{:S(2)}, u32[]{:S(2)}) collective-permute-start(bf16[272,128]{1,0:T(8,128)(2,1)S(1)} %get-tuple-element.54), channel_id=1, source_target_pairs={{0,6},{2,0},{4,2},{6,4},{1,7},{3,1},{5,3},{7,5},{8,14},{10,8},{12,... | collective-permute-start | bytes 208904 | tf_op jit(solution)/shard_map/ppermute | solution.py:33
  72.6 18.9 %all-to-all-start.1 = ((bf16[8,256,128]{2,1,0:T(8,128)(2,1)}), bf16[8,256,128]{2,1,0:T(8,128)(2,1)S(1)}, u32[]{:S(2)}, u32[]{:S(2)}) async-start(bf16[8,256,128]{2,1,0:T(8,128)(2,1)} %finish_rows.3), calls=%async_computation.1 | async-start | bytes 1048576 | tf_op jit(solution)/shard_map/all_to_all | solution.py:412
  110.1 10.7 %collective-permute-start.16 = (bf16[272,512]{1,0:T(8,128)(2,1)S(1)}, bf16[272,512]{1,0:T(8,128)(2,1)S(1)}, u32[]{:S(2)}, u32[]{:S(2)}) collective-permute-start(bf16[272,512]{1,0:T(8,128)(2,1)S(1)} %attend.5), channel_id=1, source_target_pairs={{0,16},{8,24},{16,0},{24,8},{1,17},{9,25},{17,1},{25,9},{2,18},{10... | collective-permute-start | bytes 835592 | tf_op jit(solution)/shard_map/ppermute | solution.py:33
  110.2 13.3 %collective-permute-start.17 = (bf16[272,512]{1,0:T(8,128)(2,1)S(1)}, bf16[272,512]{1,0:T(8,128)(2,1)S(1)}, u32[]{:S(2)}, u32[]{:S(2)}) collective-permute-start(bf16[272,512]{1,0:T(8,128)(2,1)S(1)} %attend.6), channel_id=1, source_target_pairs={{0,8},{8,16},{16,24},{24,0},{1,9},{9,17},{17,25},{25,1},{2,10},{10... | collective-permute-start | bytes 835592 | tf_op jit(solution)/shard_map/ppermute | solution.py:33
  110.3 13.2 %collective-permute-start.18 = (bf16[272,512]{1,0:T(8,128)(2,1)S(1)}, bf16[272,512]{1,0:T(8,128)(2,1)S(1)}, u32[]{:S(2)}, u32[]{:S(2)}) collective-permute-start(bf16[272,512]{1,0:T(8,128)(2,1)S(1)} %attend.7), channel_id=1, source_target_pairs={{0,24},{8,0},{16,8},{24,16},{1,25},{9,1},{17,9},{25,17},{2,26},{10... | collective-permute-start | bytes 835592 | tf_op jit(solution)/shard_map/ppermute | solution.py:33
  (16 other events, 56.7 us)

commit v4 on v3

--- a/solution.py
+++ b/solution.py
@@ -23,7 +23,8 @@
 NEG = -1e30
 LOG2E = math.log2(math.e)
 KEYS = 2048
-CHUNK = 512
+CHUNK = 1024
+PER = CHUNK // TOK
 ROWS_Q = GROUP * TOK
 SCALE = HEAD ** (-0.5)
 
@@ -48,93 +49,53 @@
     return jnp.where(at == 0, high, jnp.where(at == 1, row - high, 0.0)).astype(BF16)
 
 
-def head_rows(step, features, tail, weight_ref, give_ref, keep_ref):
-    rows = lax.dot_general(
-        weight_ref[...], features[...], (((1,), (1,)), ((), ())), preferred_element_type=F32
-    ).astype(BF16)
-
-    @pl.when(step < 4)
-    def to_other_core():
-        give_ref[0, :TOK, :] = rows
-        give_ref[0, TOK:, :] = tail[...]
-
-    @pl.when(step >= 4)
-    def own_core():
-        keep_ref[0, :TOK, :] = rows
-        keep_ref[0, TOK:, :] = tail[...]
-
-
-def gain_features(features, gain_ref, gained, tail):
+def head_rows(core, features, tail, weight_ref, give_ref, keep_ref):
+    for x_at in range(4):
+        for own, ref in ((0, give_ref), (1, keep_ref)):
+            head = 2 * x_at + jnp.where(own == 1, core, 1 - core)
+            weight = weight_ref[pl.ds(pl.multiple_of(head * TOK, TOK), TOK), :]
+            rows = lax.dot_general(
+                weight, features, (((1,), (1,)), ((), ())), preferred_element_type=F32
+            )
+            ref[x_at, :TOK, :] = rows.astype(BF16)
+            ref[x_at, TOK:, :] = tail
+
+
+def gain_features(features, gain_ref):
     widened = features.astype(F32)
     squares = jnp.sum(jnp.square(widened), axis=1, keepdims=True)
-    tail[...] = split_squares(squares, features.shape[0])
-    gained[...] = (widened * gain_ref[...]).astype(BF16)
-
-
-def text_project_kernel(core, hidden_ref, gain_ref, weight_ref, give_ref, keep_ref, gained, tail):
-    step = pl.program_id(0)
-
-    @pl.when(step == 0)
-    def first():
-        gain_features(hidden_ref[...], gain_ref, gained, tail)
-
-    head_rows(step, gained, tail, weight_ref, give_ref, keep_ref)
+    return (widened * gain_ref[...]).astype(BF16), split_squares(squares, features.shape[0])
+
+
+def text_project_kernel(core, hidden_ref, gain_ref, weight_ref, give_ref, keep_ref):
+    gained, tail = gain_features(hidden_ref[...], gain_ref)
+    head_rows(core[0], gained, tail, weight_ref, give_ref, keep_ref)
 
 
 def image_project_kernel(
-    core, half_ref, other_ref, proj_ref, gain_ref, weight_ref, give_ref, keep_ref, encoded, gained, tail
+    core, half_ref, other_ref, proj_ref, gain_ref, weight_ref, give_ref, keep_ref, encoded
 ):
-    step = pl.program_id(0)
-
-    @pl.when(step == 0)
-    def first():
-        @pl.when(core[0] == 0)
-        def low():
-            encoded[:HALF, :] = half_ref[...]
-            encoded[HALF:, :] = other_ref[...]
-
-        @pl.when(core[0] == 1)
-        def high():
-            encoded[:HALF, :] = other_ref[...]
-            encoded[HALF:, :] = half_ref[...]
-
-        image = jnp.dot(encoded[...], proj_ref[...], preferred_element_type=F32).astype(BF16)
-        gain_features(image, gain_ref, gained, tail)
-
-    head_rows(step, gained, tail, weight_ref, give_ref, keep_ref)
+    at = pl.multiple_of(core[0] * HALF, HALF)
+    encoded[pl.ds(at, HALF), :] = half_ref[...]
+    encoded[pl.ds(HALF - at, HALF), :] = other_ref[...]
+    image = jnp.dot(encoded[...], proj_ref[...], preferred_element_type=F32).astype(BF16)
+    gained, tail = gain_features(image, gain_ref)
+    head_rows(core[0], gained, tail, weight_ref, give_ref, keep_ref)
 
 
 def project(kernel, features, norm_gain, kv_weight, core, count, scratch):
-    whole = lambda step, core: (0, 0)
     mine = jnp.reshape(core, (1,)).astype(jnp.int32)
-
-    def head(step, core):
-        x_at = jnp.where(step < 4, step, step - 4)
-        return (2 * x_at + jnp.where(step < 4, 1 - core[0], core[0]), 0)
-
     shape = jax.ShapeDtypeStruct((4, ROWS, count), BF16)
     return pl.pallas_call(
         kernel,
         out_shape=(shape, shape),
-        grid_spec=pltpu.PrefetchScalarGridSpec(
-            num_scalar_prefetch=1,
-            grid=(8,),
-            in_specs=[
-                *[pl.BlockSpec(f.shape, whole) for f in features],
-                pl.BlockSpec((1, norm_gain.shape[0]), whole),
-                pl.BlockSpec((TOK, kv_weight.shape[1]), head),
-            ],
-            out_specs=(
-                pl.BlockSpec((1, ROWS, count), lambda step, core: (jnp.minimum(step, 3), 0, 0)),
-                pl.BlockSpec((1, ROWS, count), lambda step, core: (jnp.maximum(step, 4) - 4, 0, 0)),
-            ),
-            scratch_shapes=[
-                *scratch,
-                pltpu.VMEM((count, kv_weight.shape[1]), BF16),
-                pltpu.VMEM((16, count), BF16),
-            ],
-        ),
-        compiler_params=vmem(56),
+        in_specs=[
+            pl.BlockSpec(memory_space=pltpu.SMEM),
+            *[pl.BlockSpec(memory_space=pltpu.VMEM)] * (len(features) + 2),
+        ],
+        scratch_shapes=scratch,
+        compiler_params=vmem(8),
+        name="project",
     )(mine, *features, norm_gain[None, :], kv_weight)
 
 
@@ -207,7 +168,11 @@
                 rows = jnp.where(
                     source == float(r), image_ref[2 * r + block % 2].astype(F32), rows
                 )
-            cosine, sine = cos_ref[:, here] * (SCALE * LOG2E), sin_ref[:, here] * (SCALE * LOG2E)
+            inner_cos, inner_sin = cos_ref[:, lanes], sin_ref[:, lanes]
+            outer_cos = cos_ref[:, TOK + block : TOK + block + 1]
+            outer_sin = sin_ref[:, TOK + block : TOK + block + 1]
+            cosine = inner_cos * outer_cos - inner_sin * outer_sin
+            sine = inner_sin * outer_cos + inner_cos * outer_sin
             first, second = rows[:HALF], rows[HALF:HEAD]
             keys[:HALF, here] = (first * cosine - second * sine).astype(BF16)
             keys[HALF:, here] = (second * cosine + first * sine).astype(BF16)
@@ -226,36 +191,34 @@
     )(text, images, cosine, sine)
 
 
-def attend_kernel(step, place, keys, values, query_ref, out_ref, stacked, scores, top, mixed):
+def attend_kernel(step, place, keys, values, query_ref, out_ref, scores, top, mixed):
     z_at, y_at = place[0], place[1]
     block_at = lax.rem(y_at + step, 4)
-    for h in range(GROUP):
-        stacked[h * TOK : (h + 1) * TOK, :] = query_ref[:, h * HEAD : (h + 1) * HEAD]
     full = z_at + jnp.where(y_at < block_at, 1, 0)
     count = z_at + jnp.where(y_at <= block_at, 1, 0)
-    plain = full // 2
-    chunks = (count + 1) // 2
+    plain = full // PER
+    chunks = (count + PER - 1) // PER
     top[...] = jnp.full(top.shape, NEG, F32)
-    mixed[...] = jnp.zeros(mixed.shape, F32)
-
-    def chunk_at(chunk):
-        return pl.ds(pl.multiple_of(chunk * CHUNK, CHUNK), CHUNK)
+
+    def chunk_at(chunk, offset=0, size=CHUNK):
+        return pl.ds(pl.multiple_of(chunk * CHUNK + offset, HEAD), size)
 
     def score(chunk, masked):
-        at = chunk_at(chunk)
-        keys_now = keys[:, at]
+        keys_now = keys[:, chunk_at(chunk)]
         if masked:
             key_at = lax.broadcasted_iota(jnp.int32, (TOK, CHUNK), 1)
-            low = jnp.where(key_at < TOK, key_at, key_at - TOK + 4 * TOK)
+            key_at = key_at + (key_at // TOK) * (3 * TOK)
             query_at = lax.broadcasted_iota(jnp.int32, (TOK, CHUNK), 0)
-            offset = ((2 * chunk - z_at) * 4 + y_at - block_at) * TOK
-            allowed = low + offset <= query_at
+            offset = ((PER * chunk - z_at) * 4 + y_at - block_at) * TOK
+            allowed = key_at + offset <= query_at
         for h in range(GROUP):
             here = slice(h * TOK, (h + 1) * TOK)
-            s = jnp.dot(stacked[here, :], keys_now, preferred_element_type=F32)
+            s = jnp.dot(
+                query_ref[:, h * HEAD : (h + 1) * HEAD], keys_now, preferred_element_type=F32
+            )
             if masked:
                 s = jnp.where(allowed, s, -jnp.inf)
-            scores[here, at] = s
+            scores[here, chunk_at(chunk)] = s
             most = top[here, :]
             for lane in range(0, CHUNK, HEAD):
                 most = jnp.maximum(most, s[:, lane : lane + HEAD])
@@ -267,32 +230,50 @@
     def last():
         score(plain, True)
 
-    offset = jnp.max(top[...], axis=1, keepdims=True)
-    top[...] = jnp.broadcast_to(offset, top.shape)
-
-    @pl.loop(0, chunks)
-    def weigh(chunk):
-        at = chunk_at(chunk)
-        values_now = values[at, :]
+    top[...] = jnp.broadcast_to(jnp.max(top[...], axis=1, keepdims=True), top.shape)
+
+    def weigh(chunk, first):
+        values_now = values[chunk_at(chunk), :]
         for h in range(GROUP):
             here = slice(h * TOK, (h + 1) * TOK)
-            weights = jnp.exp2(scores[here, at] - top[here, :1]).astype(BF16)
-            mixed[here, :] += jnp.dot(weights, values_now, preferred_element_type=F32)
+            most = top[here, :]
+            weights = jnp.concatenate(
+                [
+                    jnp.exp2(scores[here, chunk_at(chunk, lane, HEAD)] - most).astype(BF16)
+                    for lane in range(0, CHUNK, HEAD)
+                ],
+                1,
+            )
+            rows = jnp.dot(weights, values_now, preferred_element_type=F32)
+            mixed[here, :] = rows if first else mixed[here, :] + rows
+
+    @pl.when(chunks > 0)
+    def some_keys():
+        weigh(0, True)
+
+    @pl.when(chunks == 0)
+    def no_keys():
+        mixed[...] = jnp.zeros(mixed.shape, F32)
+
+    pl.loop(1, chunks)(lambda chunk: weigh(chunk, False))
 
     lane = lax.broadcasted_iota(jnp.int32, (TOK, HEAD), 1)
     stats = jnp.zeros((TOK, HEAD), F32)
     for h in range(GROUP):
         here = slice(h * TOK, (h + 1) * TOK)
         total = mixed[here, HEAD:]
-        some = total > 0.0
-        safe = jnp.where(some, total, 1.0)
+        safe = jnp.where(total > 0.0, total, 1.0)
         out_ref[:TOK, h * HEAD : (h + 1) * HEAD] = (mixed[here, :HEAD] / safe).astype(BF16)
-        level = jnp.where(some, top[here, :] + jnp.log2(safe), NEG)
-        for part in range(3):
-            piece = level.astype(BF16).astype(F32)
-            stats = jnp.where(lane == 3 * h + part, piece, stats)
-            level = level - piece
-    out_ref[TOK:, :TOK] = stats.T[: ROWS - TOK].astype(BF16)
+        stats = jnp.where(lane == h, top[here, :], jnp.where(lane == GROUP + h, total, stats))
+    rows = stats.T
+    tops, totals = rows[:GROUP], rows[GROUP : 2 * GROUP]
+    some = totals > 0.0
+    level = jnp.where(some, tops + jnp.log2(jnp.where(some, totals, 1.0)), NEG)
+    high = level.astype(BF16).astype(F32)
+    middle = (level - high).astype(BF16).astype(F32)
+    low = level - high - middle
+    pad = jnp.zeros((ROWS - TOK - 3 * GROUP, TOK), F32)
+    out_ref[TOK:, :TOK] = jnp.concatenate([high, middle, low, pad], 0).astype(BF16)
     out_ref[TOK:, TOK:] = jnp.zeros((ROWS - TOK, 2 * HEAD), BF16)
 
 
@@ -305,7 +286,6 @@
             *[pl.BlockSpec(memory_space=pltpu.VMEM)] * 3,
         ],
         scratch_shapes=[
-            pltpu.VMEM((ROWS_Q, HEAD), BF16),
             pltpu.VMEM((ROWS_Q, KEYS), F32),
             pltpu.VMEM((ROWS_Q, HEAD), F32),
             pltpu.VMEM((ROWS_Q, 2 * HEAD), F32),
@@ -331,7 +311,7 @@
     for ref in parts:
         rows = ref[TOK:, :TOK].astype(F32)
         levels.append(
-            [rows[3 * h : 3 * h + 1] + rows[3 * h + 1 : 3 * h + 2] + rows[3 * h + 2 : 3 * h + 3] for h in range(GROUP)]
+            [rows[h : h + 1] + rows[4 + h : 5 + h] + rows[8 + h : 9 + h] for h in range(GROUP)]
         )
     weights = []
     for h in range(GROUP):
@@ -375,8 +355,9 @@
     x_at, core = lax.axis_index("x"), lax.axis_index("core")
 
     give, keep = project(text_project_kernel, [hidden_text], norm_gain, kv_weight, core, TOK, [])
-    patches, give, keep = lax.optimization_barrier((patches, give, keep))
     text_pieces = add_pair(keep, shift(give, "core", 1), x_at)
+    patches, text_pieces = lax.optimization_barrier((patches, text_pieces))
+    text_got = exchange(text_pieces)
 
     normed_patches = layer_norm(patches, patch_gain, patch_shift)
     enc_hidden = jax.nn.gelu(
@@ -385,8 +366,6 @@
     partial_out = jnp.dot(enc_hidden, encoder_down, preferred_element_type=F32).astype(BF16)
     halves = partial_out.reshape(2, HALF, -1)
     half = pick(halves, core).astype(F32) + shift(pick(halves, 1 - core), "core", 1).astype(F32)
-    half, text_pieces = lax.optimization_barrier((half, text_pieces))
-    text_got = exchange(text_pieces)
     sent = half.astype(BF16)
     for step in (2, 1, 3):
         half = half + shift(sent, "x", step).astype(F32)
@@ -408,16 +387,18 @@
     asked = {step: shift(queries, "y", 4 - step) for step in (2, 1, 3)}
     image_got = exchange(add_pair(keep, shift(give, "core", 1), x_at))
     image_rows = finish_rows(slot_source, image_got, TOK)
-    image_rows, text_all, asked = lax.optimization_barrier((image_rows, text_all, asked))
+    image_rows, text_all = lax.optimization_barrier((image_rows, text_all))
     images_all = lax.all_to_all(image_rows, Z, 0, 0, tiled=True)
 
     frequencies = jnp.exp(
         jnp.arange(HALF, dtype=F32) * (-2.0 * math.log(500000.0) / (2 * HALF))
     )
-    index = jnp.arange(KEYS, dtype=jnp.int32)
-    positions = ((index // TOK) * 4 + y_at) * TOK + index % TOK
+    lane = jnp.arange(TOK + HEAD, dtype=jnp.int32)
+    positions = jnp.where(lane < TOK, lane, ((lane - TOK) * 4 + y_at) * TOK)
     angles = positions.astype(F32)[None, :] * frequencies[:, None]
-    keys, values = merge(text_all, images_all, jnp.cos(angles), jnp.sin(angles))
+    factor = jnp.where(lane < TOK, SCALE * LOG2E, 1.0)[None, :]
+    tables = (jnp.cos(angles) * factor, jnp.sin(angles) * factor)
+    keys, values = merge(text_all, images_all, *tables)
     place = jnp.stack([z_at, y_at]).astype(jnp.int32)
     received = []
     for step in (2, 1, 3):

time: 126 us -> 115 us (0.913)
  the two profiles are of different devices: /device:TPU:198 before, /device:TPU:220 now
where the time goes in v4:
time: 115 us
  waiting for transfers between devices  42.7 us (37%)
  starting transfers between devices  32.2 us (28%)
  Pallas kernels  24.7 us (21%)
  local copies, waits for them, and re-layouts  9.81 us (9%)
  matrix products  3.03 us (3%)
  other arithmetic  2.05 us (2%)
    ppermute x19, waiting for transfers between devices, shift(): lax.ppermute(values, axis, [(i, (i + step) % count) for i in range(count)])  24.1 us
    ppermute x19, starting transfers between devices, shift(): lax.ppermute(values, axis, [(i, (i + step) % count) for i in range(count)])  18.7 us
    pallas_call x4, Pallas kernels, attend(): pl.pallas_call(functools.partial(attend_kernel, step), out_shape=jax.Shap...  17.8 us
    unnamed x28, local copies, waits for them, and re-layouts  9.79 us
    all_to_all x1, waiting for transfers between devices, body(): text_all = lax.all_to_all(text_rows, Z, 0, 0, tiled=True)  9.38 us
    all_to_all x1, waiting for transfers between devices, body(): images_all = lax.all_to_all(image_rows, Z, 0, 0, tiled=True)  9.21 us
    all_to_all x1, starting transfers between devices, body(): images_all = lax.all_to_all(image_rows, Z, 0, 0, tiled=True)  7.26 us
    all_to_all x1, starting transfers between devices, body(): text_all = lax.all_to_all(text_rows, Z, 0, 0, tiled=True)  6.3 us
  transfers between devices with their start and end apart: 21, of which 11 were waited for; matrix products, arithmetic and copies ran while one was open for 0% of the time, Pallas kernels for 19%

profile of v4, /device:TPU:220, one launch (start us, length us, event | category | flops | bytes accessed | tf_op | source)
XLA Modules:
  0.0 114.8 jit_solution(11576482704935093380)
XLA Ops:
  0.0 2.3 %copy-done.1 = bf16[2048,1024]{1,0:T(8,128)(2,1)S(1)} copy-done((bf16[2048,1024]{1,0:T(8,128)(2,1)S(1)}, bf16[2048,1024]{1,0:T(8,128)(2,1)}, u32[]{:S(2)}) %copy-start.1) | copy-done | bytes 4194328
  5.5 1.9 %collective-permute-done.got_ref = bf16[4,272,256]{2,1,0:T(8,128)(2,1)S(1)} collective-permute-done((bf16[4,272,256]{2,1,0:T(8,128)(2,1)S(1)}, bf16[4,272,256]{2,1,0:T(8,128)(2,1)S(1)}, u32[]{:S(2)}, u32[]{:S(2)}) %collective-permute-start) | collective-permute-done | bytes 557088 | tf_op jit(solution)/shard_map/ppermute | solution.py:34
  9.0 3.0 %convolution_convert_fusion = bf16[128,1280]{1,0:T(8,128)(2,1)S(1)} fusion(bf16[640,1280]{1,0:T(8,128)(2,1)S(1)} %copy-done, bf16[1280,640]{1,0:T(8,128)(2,1)} %param.14, bf16[128,1280]{1,0:T(8,128)(2,1)} %param.11, f32[1280]{0:T(1024)S(1)} %copy-done.12, f32[1280]{0:T(1024)S(1)} %copy-done.13, f32[128]{0:T(128)S(1)} %add_rsqrt_fusion, ...), kind=kOutput, calls=%fused_computation | convolution fusion | flops 425902080 | bytes 3943424 | tf_op jit(solution)/shard_map/dot_general | solution.py:366
  13.6 1.5 %collective-permute-start.4 = (bf16[64,1280]{1,0:T(8,128)(2,1)S(1)}, bf16[64,1280]{1,0:T(8,128)(2,1)S(1)}, u32[]{:S(2)}, u32[]{:S(2)}) collective-permute-start(bf16[64,1280]{1,0:T(8,128)(2,1)S(1)} %fusion.27), channel_id=1, source_target_pairs={{0,6},{2,0},{4,2},{6,4},{1,7},{3,1},{5,3},{7,5},{8,14},{10,8},{12,... | collective-permute-start | bytes 491528 | tf_op jit(solution)/shard_map/ppermute | solution.py:34
  15.7 2.3 %collective-permute-start.2 = (bf16[64,1280]{1,0:T(8,128)(2,1)S(1)}, bf16[64,1280]{1,0:T(8,128)(2,1)S(1)}, u32[]{:S(2)}, u32[]{:S(2)}) collective-permute-start(bf16[64,1280]{1,0:T(8,128)(2,1)S(1)} %fusion.27), channel_id=1, source_target_pairs={{0,4},{2,6},{4,0},{6,2},{1,5},{3,7},{5,1},{7,3},{8,12},{10,14},{12... | collective-permute-start | bytes 491528 | tf_op jit(solution)/shard_map/ppermute | solution.py:34
  20.8 8.9 %collective-permute-done.6.refs_2_ = bf16[272,256]{1,0:T(8,128)(2,1)S(1)} collective-permute-done((bf16[272,256]{1,0:T(8,128)(2,1)S(1)}, bf16[272,256]{1,0:T(8,128)(2,1)S(1)}, u32[]{:S(2)}, u32[]{:S(2)}) %collective-permute-start.6) | collective-permute-done | bytes 139296 | tf_op jit(solution)/shard_map/ppermute | solution.py:34
  31.5 6.3 %all-to-all-start = ((bf16[8,272,256]{2,1,0:T(8,128)(2,1)}), bf16[8,272,256]{2,1,0:T(8,128)(2,1)S(1)}, u32[]{:S(2)}, u32[]{:S(2)}) async-start(bf16[8,272,256]{2,1,0:T(8,128)(2,1)} %copy-done.3), calls=%async_computation | async-start | bytes 2228224 | tf_op jit(solution)/shard_map/all_to_all | solution.py:375
  39.3 2.2 %copy-done.2 = bf16[2048,1024]{1,0:T(8,128)(2,1)S(1)} copy-done((bf16[2048,1024]{1,0:T(8,128)(2,1)S(1)}, bf16[2048,1024]{1,0:T(8,128)(2,1)}, u32[]{:S(2)}) %copy-start.2) | copy-done | bytes 4194328
  41.4 1.7 %copy-done.4 = bf16[1280,1024]{1,0:T(8,128)(2,1)S(1)} copy-done((bf16[1280,1024]{1,0:T(8,128)(2,1)S(1)}, bf16[1280,1024]{1,0:T(8,128)(2,1)}, u32[]{:S(2)}) %copy-start.4) | copy-done | bytes 2621464
  43.2 1.6 %project.3 = (bf16[4,272,128]{2,1,0:T(8,128)(2,1)S(1)}, bf16[4,272,128]{2,1,0:T(8,128)(2,1)S(1)}) custom-call(s32[1]{0:T(128)} %bitcast.3.core, bf16[64,1280]{1,0:T(8,128)(2,1)S(1)} %fusion.11.half_ref, bf16[64,1280]{1,0:T(8,128)(2,1)S(1)} %collective-permute-done.8.other_ref, bf16[1280,1024]{1,0:T(8,128)(2,1)S(1)} %copy-done.4, f32[1,1024]{1,0:T(1,128)S(1)} %bitcast.19, ...), custom_call_target="tpu_custom_call" | custom-call | tf_op jit(solution)/shard_map/project/pallas_call | solution.py:89
  45.0 1.4 %collective-permute-done.9.got_ref = bf16[4,272,128]{2,1,0:T(8,128)(2,1)S(1)} collective-permute-done((bf16[4,272,128]{2,1,0:T(8,128)(2,1)S(1)}, bf16[4,272,128]{2,1,0:T(8,128)(2,1)S(1)}, u32[]{:S(2)}, u32[]{:S(2)}) %collective-permute-start.9) | collective-permute-done | bytes 278560 | tf_op jit(solution)/shard_map/ppermute | solution.py:34
  47.6 1.7 %collective-permute-start.11 = (bf16[272,128]{1,0:T(8,128)(2,1)S(1)}, bf16[272,128]{1,0:T(8,128)(2,1)S(1)}, u32[]{:S(2)}, u32[]{:S(2)}) collective-permute-start(bf16[272,128]{1,0:T(8,128)(2,1)S(1)} %get-tuple-element.44), channel_id=1, source_target_pairs={{0,2},{2,4},{4,6},{6,0},{1,3},{3,5},{5,7},{7,1},{8,10},{10,12},{12... | collective-permute-start | bytes 208904 | tf_op jit(solution)/shard_map/ppermute | solution.py:34
  49.6 3.4 %collective-permute-done.10.refs_1_ = bf16[272,128]{1,0:T(8,128)(2,1)S(1)} collective-permute-done((bf16[272,128]{1,0:T(8,128)(2,1)S(1)}, bf16[272,128]{1,0:T(8,128)(2,1)S(1)}, u32[]{:S(2)}, u32[]{:S(2)}) %collective-permute-start.10) | collective-permute-done | bytes 69664 | tf_op jit(solution)/shard_map/ppermute | solution.py:34
  55.0 9.4 %all-to-all-done.text_ref = bf16[8,272,256]{2,1,0:T(8,128)(2,1)S(1)} async-done(((bf16[8,272,256]{2,1,0:T(8,128)(2,1)}), bf16[8,272,256]{2,1,0:T(8,128)(2,1)S(1)}, u32[]{:S(2)}, u32[]{:S(2)}) %all-to-all-start) | async-done | bytes 1114144 | tf_op jit(solution)/shard_map/all_to_all | solution.py:375
  64.4 7.3 %all-to-all-start.1 = ((bf16[8,256,128]{2,1,0:T(8,128)(2,1)}), bf16[8,256,128]{2,1,0:T(8,128)(2,1)S(1)}, u32[]{:S(2)}, u32[]{:S(2)}) async-start(bf16[8,256,128]{2,1,0:T(8,128)(2,1)} %copy-done.5), calls=%async_computation.1 | async-start | bytes 1048576 | tf_op jit(solution)/shard_map/all_to_all | solution.py:391
  72.9 3.2 %collective-permute-start.17 = (bf16[256,512]{1,0:T(8,128)(2,1)}, bf16[256,512]{1,0:T(8,128)(2,1)}, u32[]{:S(2)}, u32[]{:S(2)}) collective-permute-start(bf16[256,512]{1,0:T(8,128)(2,1)} %query_ref.1), channel_id=1, source_target_pairs={{0,8},{8,16},{16,24},{24,0},{1,9},{9,17},{17,25},{25,1},{2,10},{10... | collective-permute-start | bytes 786440 | tf_op jit(solution)/shard_map/ppermute | solution.py:34
  76.7 9.2 %all-to-all-done.1.image_ref = bf16[8,256,128]{2,1,0:T(8,128)(2,1)S(1)} async-done(((bf16[8,256,128]{2,1,0:T(8,128)(2,1)}), bf16[8,256,128]{2,1,0:T(8,128)(2,1)S(1)}, u32[]{:S(2)}, u32[]{:S(2)}) %all-to-all-start.1) | async-done | bytes 524320 | tf_op jit(solution)/shard_map/all_to_all | solution.py:391
  86.9 4.5 %attend.5 = bf16[272,512]{1,0:T(8,128)(2,1)S(1)} custom-call(s32[2]{0:T(128)S(1)} %pad_add_fusion.place, bf16[128,2048]{1,0:T(8,128)(2,1)S(1)} %get-tuple-element.49.keys, bf16[2048,256]{1,0:T(8,128)(2,1)S(1)} %get-tuple-element.50.values, bf16[256,512]{1,0:T(8,128)(2,1)} %collective-permute-done.13.query_ref), custom_call_target="tpu_custom_call" | custom-call | flops 1073741824 | bytes 2097152 | tf_op jit(solution)/shard_map/attend/pallas_call | solution.py:281
  92.7 4.5 %attend.6 = bf16[272,512]{1,0:T(8,128)(2,1)S(1)} custom-call(s32[2]{0:T(128)S(1)} %pad_add_fusion.place, bf16[128,2048]{1,0:T(8,128)(2,1)S(1)} %get-tuple-element.49.keys, bf16[2048,256]{1,0:T(8,128)(2,1)S(1)} %get-tuple-element.50.values, bf16[256,512]{1,0:T(8,128)(2,1)} %collective-permute-done.15.query_ref), custom_call_target="tpu_custom_call" | custom-call | flops 1073741824 | bytes 2097152 | tf_op jit(solution)/shard_map/attend/pallas_call | solution.py:281
  97.2 2.5 %collective-permute-start.16 = (bf16[272,512]{1,0:T(8,128)(2,1)S(1)}, bf16[272,512]{1,0:T(8,128)(2,1)S(1)}, u32[]{:S(2)}, u32[]{:S(2)}) collective-permute-start(bf16[272,512]{1,0:T(8,128)(2,1)S(1)} %attend.6), channel_id=1, source_target_pairs={{0,8},{8,16},{16,24},{24,0},{1,9},{9,17},{17,25},{25,1},{2,10},{10... | collective-permute-start | bytes 835592 | tf_op jit(solution)/shard_map/ppermute | solution.py:34
  99.6 4.5 %attend.7 = bf16[272,512]{1,0:T(8,128)(2,1)S(1)} custom-call(s32[2]{0:T(128)S(1)} %pad_add_fusion.place, bf16[128,2048]{1,0:T(8,128)(2,1)S(1)} %get-tuple-element.49.keys, bf16[2048,256]{1,0:T(8,128)(2,1)S(1)} %get-tuple-element.50.values, bf16[256,512]{1,0:T(8,128)(2,1)} %collective-permute-done.17.query_ref), custom_call_target="tpu_custom_call" | custom-call | flops 1073741824 | bytes 2097152 | tf_op jit(solution)/shard_map/attend/pallas_call | solution.py:281
  104.2 4.5 %attend.4.refs_0_ = bf16[272,512]{1,0:T(8,128)(2,1)S(1)} custom-call(s32[2]{0:T(128)S(1)} %pad_add_fusion.place, bf16[128,2048]{1,0:T(8,128)(2,1)S(1)} %get-tuple-element.49.keys, bf16[2048,256]{1,0:T(8,128)(2,1)S(1)} %get-tuple-element.50.values, bf16[256,512]{1,0:T(8,128)(2,1)} %query_ref.1), custom_call_target="tpu_custom_call" | custom-call | flops 1073741824 | bytes 2097152 | tf_op jit(solution)/shard_map/attend/pallas_call | solution.py:281
  108.7 4.6 %collective-permute-done.18.refs_3_ = bf16[272,512]{1,0:T(8,128)(2,1)S(1)} collective-permute-done((bf16[272,512]{1,0:T(8,128)(2,1)S(1)}, bf16[272,512]{1,0:T(8,128)(2,1)S(1)}, u32[]{:S(2)}, u32[]{:S(2)}) %collective-permute-start.18) | collective-permute-done | bytes 278560 | tf_op jit(solution)/shard_map/ppermute | solution.py:34
  113.3 1.5 %combine.1 = bf16[256,512]{1,0:T(8,128)(2,1)} custom-call(bf16[272,512]{1,0:T(8,128)(2,1)S(1)} %attend.4.refs_0_, bf16[272,512]{1,0:T(8,128)(2,1)S(1)} %collective-permute-done.14.refs_1_, bf16[272,512]{1,0:T(8,128)(2,1)S(1)} %collective-permute-done.16.refs_2_, bf16[272,512]{1,0:T(8,128)(2,1)S(1)} %collective-permute-done.18.refs_3_), custom_call_target="tpu_custom_call" | custom-call | tf_op jit(solution)/shard_map/combine/pallas_call | solution.py:333
  (71 shorter events, 20.7 us)
Async XLA Ops:
  0.0 8.9 %copy-start = (bf16[640,1280]{1,0:T(8,128)(2,1)S(1)}, bf16[640,1280]{1,0:T(8,128)(2,1)}, u32[]{:S(2)}) copy-start(bf16[640,1280]{1,0:T(8,128)(2,1)} %param.15) | copy-start | bytes 4915204
  5.4 2.0 %collective-permute-start = (bf16[4,272,256]{2,1,0:T(8,128)(2,1)S(1)}, bf16[4,272,256]{2,1,0:T(8,128)(2,1)S(1)}, u32[]{:S(2)}, u32[]{:S(2)}) collective-permute-start(bf16[4,272,256]{2,1,0:T(8,128)(2,1)S(1)} %get-tuple-element.29), channel_id=1, source_target_pairs={{0,1},{1,0},{2,3},{3,2},{4,5},{5,4},{6,7},{7,6},{8,9},{9,8},{10,11... | collective-permute-start | bytes 1671176 | tf_op jit(solution)/shard_map/ppermute | solution.py:34
  8.9 20.8 %copy-start.9 = (s32[2]{0:T(128)S(1)}, s32[2]{0:T(128)}, u32[]{:S(2)}) copy-start(s32[2]{0:T(128)} %slots.3) | copy-start | bytes 28
  12.0 19.4 %copy-start.11 = (bf16[128,1280]{1,0:T(8,128)(2,1)S(1)}, bf16[128,1280]{1,0:T(8,128)(2,1)}, u32[]{:S(2)}) copy-start(bf16[128,1280]{1,0:T(8,128)(2,1)} %param.11) | copy-start | bytes 983044
  12.0 1.5 %collective-permute-start.1 = (bf16[64,1280]{1,0:T(8,128)(2,1)S(1)}, bf16[64,1280]{1,0:T(8,128)(2,1)S(1)}, u32[]{:S(2)}, u32[]{:S(2)}) collective-permute-start(bf16[64,1280]{1,0:T(8,128)(2,1)S(1)} %dynamic-slice_bitcast_fusion), channel_id=1, source_target_pairs={{0,1},{1,0},{2,3},{3,2},{4,5},{5,4},{6,7},{7,6},{8,9},{9,8},{10,11... | collective-permute-start | bytes 491528 | tf_op jit(solution)/shard_map/ppermute | solution.py:34
  12.2 8.0 %collective-permute-start.5 = (bf16[272,256]{1,0:T(8,128)(2,1)S(1)}, bf16[272,256]{1,0:T(8,128)(2,1)S(1)}, u32[]{:S(2)}, u32[]{:S(2)}) collective-permute-start(bf16[272,256]{1,0:T(8,128)(2,1)S(1)} %get-tuple-element.36), channel_id=1, source_target_pairs={{0,4},{2,6},{4,0},{6,2},{1,5},{3,7},{5,1},{7,3},{8,12},{10,14},{12... | collective-permute-start | bytes 417800 | tf_op jit(solution)/shard_map/ppermute | solution.py:34
  13.6 17.8 %collective-permute-start.4 = (bf16[64,1280]{1,0:T(8,128)(2,1)S(1)}, bf16[64,1280]{1,0:T(8,128)(2,1)S(1)}, u32[]{:S(2)}, u32[]{:S(2)}) collective-permute-start(bf16[64,1280]{1,0:T(8,128)(2,1)S(1)} %fusion.27), channel_id=1, source_target_pairs={{0,6},{2,0},{4,2},{6,4},{1,7},{3,1},{5,3},{7,5},{8,14},{10,8},{12,... | collective-permute-start | bytes 491528 | tf_op jit(solution)/shard_map/ppermute | solution.py:34
  15.0 16.3 %collective-permute-start.3 = (bf16[64,1280]{1,0:T(8,128)(2,1)S(1)}, bf16[64,1280]{1,0:T(8,128)(2,1)S(1)}, u32[]{:S(2)}, u32[]{:S(2)}) collective-permute-start(bf16[64,1280]{1,0:T(8,128)(2,1)S(1)} %fusion.27), channel_id=1, source_target_pairs={{0,2},{2,4},{4,6},{6,0},{1,3},{3,5},{5,7},{7,1},{8,10},{10,12},{12... | collective-permute-start | bytes 491528 | tf_op jit(solution)/shard_map/ppermute | solution.py:34
  15.7 15.7 %collective-permute-start.2 = (bf16[64,1280]{1,0:T(8,128)(2,1)S(1)}, bf16[64,1280]{1,0:T(8,128)(2,1)S(1)}, u32[]{:S(2)}, u32[]{:S(2)}) collective-permute-start(bf16[64,1280]{1,0:T(8,128)(2,1)S(1)} %fusion.27), channel_id=1, source_target_pairs={{0,4},{2,6},{4,0},{6,2},{1,5},{3,7},{5,1},{7,3},{8,12},{10,14},{12... | collective-permute-start | bytes 491528 | tf_op jit(solution)/shard_map/ppermute | solution.py:34
  18.0 11.8 %collective-permute-start.6 = (bf16[272,256]{1,0:T(8,128)(2,1)S(1)}, bf16[272,256]{1,0:T(8,128)(2,1)S(1)}, u32[]{:S(2)}, u32[]{:S(2)}) collective-permute-start(bf16[272,256]{1,0:T(8,128)(2,1)S(1)} %get-tuple-element.37), channel_id=1, source_target_pairs={{0,2},{2,4},{4,6},{6,0},{1,3},{3,5},{5,7},{7,1},{8,10},{10,12},{12... | collective-permute-start | bytes 417800 | tf_op jit(solution)/shard_map/ppermute | solution.py:34
  20.3 9.4 %collective-permute-start.7 = (bf16[272,256]{1,0:T(8,128)(2,1)S(1)}, bf16[272,256]{1,0:T(8,128)(2,1)S(1)}, u32[]{:S(2)}, u32[]{:S(2)}) collective-permute-start(bf16[272,256]{1,0:T(8,128)(2,1)S(1)} %get-tuple-element.38), channel_id=1, source_target_pairs={{0,6},{2,0},{4,2},{6,4},{1,7},{3,1},{5,3},{7,5},{8,14},{10,8},{12,... | collective-permute-start | bytes 417800 | tf_op jit(solution)/shard_map/ppermute | solution.py:34
  31.5 32.8 %all-to-all-start = ((bf16[8,272,256]{2,1,0:T(8,128)(2,1)}), bf16[8,272,256]{2,1,0:T(8,128)(2,1)S(1)}, u32[]{:S(2)}, u32[]{:S(2)}) async-start(bf16[8,272,256]{2,1,0:T(8,128)(2,1)} %copy-done.3), calls=%async_computation | async-start | bytes 2228224 | tf_op jit(solution)/shard_map/all_to_all | solution.py:375
  37.9 1.4 %collective-permute-start.8 = (bf16[64,1280]{1,0:T(8,128)(2,1)S(1)}, bf16[64,1280]{1,0:T(8,128)(2,1)S(1)}, u32[]{:S(2)}, u32[]{:S(2)}) collective-permute-start(bf16[64,1280]{1,0:T(8,128)(2,1)S(1)} %fusion.11.half_ref), channel_id=1, source_target_pairs={{0,1},{1,0},{2,3},{3,2},{4,5},{5,4},{6,7},{7,6},{8,9},{9,8},{10,11... | collective-permute-start | bytes 491528 | tf_op jit(solution)/shard_map/ppermute | solution.py:34
  44.8 1.6 %collective-permute-start.9 = (bf16[4,272,128]{2,1,0:T(8,128)(2,1)S(1)}, bf16[4,272,128]{2,1,0:T(8,128)(2,1)S(1)}, u32[]{:S(2)}, u32[]{:S(2)}) collective-permute-start(bf16[4,272,128]{2,1,0:T(8,128)(2,1)S(1)} %get-tuple-element.41), channel_id=1, source_target_pairs={{0,1},{1,0},{2,3},{3,2},{4,5},{5,4},{6,7},{7,6},{8,9},{9,8},{10,11... | collective-permute-start | bytes 835592 | tf_op jit(solution)/shard_map/ppermute | solution.py:34
  46.5 6.6 %collective-permute-start.10 = (bf16[272,128]{1,0:T(8,128)(2,1)S(1)}, bf16[272,128]{1,0:T(8,128)(2,1)S(1)}, u32[]{:S(2)}, u32[]{:S(2)}) collective-permute-start(bf16[272,128]{1,0:T(8,128)(2,1)S(1)} %get-tuple-element.43), channel_id=1, source_target_pairs={{0,4},{2,6},{4,0},{6,2},{1,5},{3,7},{5,1},{7,3},{8,12},{10,14},{12... | collective-permute-start | bytes 208904 | tf_op jit(solution)/shard_map/ppermute | solution.py:34
  47.6 5.5 %collective-permute-start.11 = (bf16[272,128]{1,0:T(8,128)(2,1)S(1)}, bf16[272,128]{1,0:T(8,128)(2,1)S(1)}, u32[]{:S(2)}, u32[]{:S(2)}) collective-permute-start(bf16[272,128]{1,0:T(8,128)(2,1)S(1)} %get-tuple-element.44), channel_id=1, source_target_pairs={{0,2},{2,4},{4,6},{6,0},{1,3},{3,5},{5,7},{7,1},{8,10},{10,12},{12... | collective-permute-start | bytes 208904 | tf_op jit(solution)/shard_map/ppermute | solution.py:34
  49.3 4.3 %collective-permute-start.12 = (bf16[272,128]{1,0:T(8,128)(2,1)S(1)}, bf16[272,128]{1,0:T(8,128)(2,1)S(1)}, u32[]{:S(2)}, u32[]{:S(2)}) collective-permute-start(bf16[272,128]{1,0:T(8,128)(2,1)S(1)} %get-tuple-element.45), channel_id=1, source_target_pairs={{0,6},{2,0},{4,2},{6,4},{1,7},{3,1},{5,3},{7,5},{8,14},{10,8},{12,... | collective-permute-start | bytes 208904 | tf_op jit(solution)/shard_map/ppermute | solution.py:34
  64.4 21.5 %all-to-all-start.1 = ((bf16[8,256,128]{2,1,0:T(8,128)(2,1)}), bf16[8,256,128]{2,1,0:T(8,128)(2,1)S(1)}, u32[]{:S(2)}, u32[]{:S(2)}) async-start(bf16[8,256,128]{2,1,0:T(8,128)(2,1)} %copy-done.5), calls=%async_computation.1 | async-start | bytes 1048576 | tf_op jit(solution)/shard_map/all_to_all | solution.py:391
  71.6 15.3 %collective-permute-start.13 = (bf16[256,512]{1,0:T(8,128)(2,1)}, bf16[256,512]{1,0:T(8,128)(2,1)}, u32[]{:S(2)}, u32[]{:S(2)}) collective-permute-start(bf16[256,512]{1,0:T(8,128)(2,1)} %query_ref.1), channel_id=1, source_target_pairs={{0,16},{8,24},{16,0},{24,8},{1,17},{9,25},{17,1},{25,9},{2,18},{10... | collective-permute-start | bytes 786440 | tf_op jit(solution)/shard_map/ppermute | solution.py:34
  72.9 19.8 %collective-permute-start.15 = (bf16[256,512]{1,0:T(8,128)(2,1)}, bf16[256,512]{1,0:T(8,128)(2,1)}, u32[]{:S(2)}, u32[]{:S(2)}) collective-permute-start(bf16[256,512]{1,0:T(8,128)(2,1)} %query_ref.1), channel_id=1, source_target_pairs={{0,24},{8,0},{16,8},{24,16},{1,25},{9,1},{17,9},{25,17},{2,26},{10... | collective-permute-start | bytes 786440 | tf_op jit(solution)/shard_map/ppermute | solution.py:34
  72.9 26.8 %collective-permute-start.17 = (bf16[256,512]{1,0:T(8,128)(2,1)}, bf16[256,512]{1,0:T(8,128)(2,1)}, u32[]{:S(2)}, u32[]{:S(2)}) collective-permute-start(bf16[256,512]{1,0:T(8,128)(2,1)} %query_ref.1), channel_id=1, source_target_pairs={{0,8},{8,16},{16,24},{24,0},{1,9},{9,17},{17,25},{25,1},{2,10},{10... | collective-permute-start | bytes 786440 | tf_op jit(solution)/shard_map/ppermute | solution.py:34
  91.4 17.3 %collective-permute-start.14 = (bf16[272,512]{1,0:T(8,128)(2,1)S(1)}, bf16[272,512]{1,0:T(8,128)(2,1)S(1)}, u32[]{:S(2)}, u32[]{:S(2)}) collective-permute-start(bf16[272,512]{1,0:T(8,128)(2,1)S(1)} %attend.5), channel_id=1, source_target_pairs={{0,16},{8,24},{16,0},{24,8},{1,17},{9,25},{17,1},{25,9},{2,18},{10... | collective-permute-start | bytes 835592 | tf_op jit(solution)/shard_map/ppermute | solution.py:34
  97.2 11.5 %collective-permute-start.16 = (bf16[272,512]{1,0:T(8,128)(2,1)S(1)}, bf16[272,512]{1,0:T(8,128)(2,1)S(1)}, u32[]{:S(2)}, u32[]{:S(2)}) collective-permute-start(bf16[272,512]{1,0:T(8,128)(2,1)S(1)} %attend.6), channel_id=1, source_target_pairs={{0,8},{8,16},{16,24},{24,0},{1,9},{9,17},{17,25},{25,1},{2,10},{10... | collective-permute-start | bytes 835592 | tf_op jit(solution)/shard_map/ppermute | solution.py:34
  104.1 9.2 %collective-permute-start.18 = (bf16[272,512]{1,0:T(8,128)(2,1)S(1)}, bf16[272,512]{1,0:T(8,128)(2,1)S(1)}, u32[]{:S(2)}, u32[]{:S(2)}) collective-permute-start(bf16[272,512]{1,0:T(8,128)(2,1)S(1)} %attend.7), channel_id=1, source_target_pairs={{0,24},{8,0},{16,8},{24,16},{1,25},{9,1},{17,9},{25,17},{2,26},{10... | collective-permute-start | bytes 835592 | tf_op jit(solution)/shard_map/ppermute | solution.py:34
  (11 other events, 27.9 us)
